TPU v7x, 256 devices: a whole 4x4x8 slice. The times are simulated.
256 devices in a mesh: slab: 64 (over y, z, core), batch: 4 (over x).
Axes of the slice: x: 4, y: 4, z: 8, core: 2. Of those that a mesh axis runs over, the one named last changes fastest.
Arguments:
- fields: bfloat16 [4, 32, 256, 128, 128], P('batch', None, 'slab'), may hold values from -6 to 6
- cotangent: bfloat16 [4, 32, 256, 128, 128], P('batch', None, 'slab'), may hold values from -6 to 6
- local_weight: bfloat16 [32, 32], replicated, may hold values from -1 to 1
- spectral_weight: bfloat16 [2, 32, 32, 16384], P(None, None, None, ('slab', 'batch')), may hold values from -4 to 4
Outputs:
- field_grad: bfloat16 [4, 32, 256, 128, 128], P('batch', None, 'slab')
- weight_grad: float32 [2, 32, 32, 16384], P(None, None, None, ('slab', 'batch'))
All inputs are finite; a program needn't handle non-finite values.
Results may differ from a plain program's by a relative error of at most 0.023.
Values may be sent and summed in bfloat16 or wider, within the bound.
A program may use at most 128 MiB of HBM per device.

v0:
```python
from functools import partial
import math

import jax
import jax.numpy as jnp
from jax import lax
from jax.sharding import PartitionSpec as P

C = 32
NY = 128
NZ = 128
MX = 32
MY = 32
MZ = 16


def frequencies(number, signed):
    counter = jnp.arange(number, dtype=jnp.int32)
    if signed:
        return jnp.where(counter < number // 2, counter, counter - number)
    return counter


def wave_table(number, length, signed):
    wave_numbers = frequencies(number, signed)
    positions = jnp.arange(length, dtype=jnp.int32)
    phases = jnp.mod(wave_numbers[:, None] * positions[None, :], length).astype(jnp.float32)
    angles = phases * (2.0 * math.pi / length)
    return (jnp.cos(angles), jnp.sin(angles))


def forward_pair(cos_table, sin_table):
    cos_rows = cos_table.T
    sin_rows = sin_table.T
    return jnp.stack(
        [jnp.stack([cos_rows, -sin_rows], 1), jnp.stack([sin_rows, cos_rows], 1)], 1
    ).astype(jnp.bfloat16)


def inverse_pair(cos_table, sin_table):
    return jnp.stack(
        [jnp.stack([cos_table, sin_table], 1), jnp.stack([-sin_table, cos_table], 1)], 1
    ).astype(jnp.bfloat16)


def make_tables(length_x):
    cos_y, sin_y = wave_table(MY, NY, True)
    cos_z, sin_z = wave_table(MZ, NZ, False)
    cos_x, sin_x = wave_table(MX, length_x, True)
    analysis_y = jnp.stack([cos_y.T, -sin_y.T], 1).astype(jnp.bfloat16)
    final_y = jnp.stack([cos_y, -sin_y], 0).astype(jnp.bfloat16)
    return (
        analysis_y,
        forward_pair(cos_z, sin_z),
        forward_pair(cos_x, sin_x),
        inverse_pair(cos_x, sin_x),
        inverse_pair(cos_z, sin_z),
        final_y,
    )


def contract(formula, left, right):
    return jnp.einsum(formula, left, right, preferred_element_type=jnp.float32)


def analyse(field, tables, offset):
    analysis_y, pair_z, pair_x = (tables[0], tables[1], tables[2])
    first = contract("bcxyz,ypk->bcxpkz", field, analysis_y).astype(jnp.bfloat16)
    second = contract("bcxpyz,zpqk->bcxqyk", first, pair_z).astype(jnp.bfloat16)
    samples, channels, width_x = (second.shape[0], second.shape[1], second.shape[2])
    second = second.reshape(samples, channels, width_x, 2, MY * MZ)
    rows = lax.dynamic_slice_in_dim(pair_x, offset, width_x, 0)
    partial_sum = contract("bcxpm,xpqk->bcqmk", second, rows)
    partial_sum = partial_sum.reshape(samples, channels, 2, MY * MZ * MX)
    result = lax.psum_scatter(partial_sum, "slab", scatter_dimension=3, tiled=True)
    return result


def synthesise(modes_part, tables, offset, width_x):
    back_x, back_z, final_y = (tables[3], tables[4], tables[5])
    samples, channels = (modes_part.shape[0], modes_part.shape[1])
    whole = lax.all_gather(modes_part, "slab", axis=3, tiled=True)
    grid = whole.reshape(samples, channels, 2, MY * MZ, MX)
    columns = lax.dynamic_slice_in_dim(back_x, offset, width_x, 3)
    first = contract("bcpmk,kpqx->bcxqm", grid, columns).astype(jnp.bfloat16)
    first = first.reshape(samples, channels, width_x, 2, MY, MZ)
    second = contract("bcxpyk,kpqz->bcxqyz", first, back_z).astype(jnp.bfloat16)
    return contract("bcxpkz,pky->bcxyz", second, final_y)


def spectral_mix(values, weights):
    product = partial(jnp.einsum, precision=lax.Precision.HIGHEST)
    real_w = weights[0].astype(jnp.float32)
    imag_w = weights[1].astype(jnp.float32)
    real_v = values[:, :, 0]
    imag_v = values[:, :, 1]
    out_real = product("sck,cok->sok", real_v, real_w) - product("sck,cok->sok", imag_v, imag_w)
    out_imag = product("sck,cok->sok", imag_v, real_w) + product("sck,cok->sok", real_v, imag_w)
    return jnp.stack([out_real, out_imag], 2).astype(jnp.bfloat16)


def spectral_adjoint(grads, values, weights):
    product = partial(jnp.einsum, precision=lax.Precision.HIGHEST)
    real_w = weights[0].astype(jnp.float32)
    imag_w = weights[1].astype(jnp.float32)
    real_g = grads[:, :, 0]
    imag_g = grads[:, :, 1]
    real_v = values[:, :, 0]
    imag_v = values[:, :, 1]
    grad_real = product("sok,sck->cok", real_g, real_v) + product("sok,sck->cok", imag_g, imag_v)
    grad_imag = product("sok,sck->cok", imag_g, real_v) - product("sok,sck->cok", real_g, imag_v)
    back_real = product("cok,sok->sck", real_w, real_g) + product("cok,sok->sck", imag_w, imag_g)
    back_imag = product("cok,sok->sck", real_w, imag_g) - product("cok,sok->sck", imag_w, real_g)
    return (
        jnp.stack([grad_real, grad_imag], 0),
        jnp.stack([back_real, back_imag], 2).astype(jnp.bfloat16),
    )


def gelu_slope(values):
    normal_cdf = 0.5 * (1.0 + jax.scipy.special.erf(values / math.sqrt(2.0)))
    density = jnp.exp(-0.5 * values * values) / math.sqrt(2.0 * math.pi)
    return normal_cdf + values * density


def body(fields, cotangent, local_weight, spectral_weight):
    width_x = fields.shape[2]
    length_x = width_x * lax.axis_size("slab")
    tables = make_tables(length_x)
    offset = lax.axis_index("slab") * width_x
    scale_in = 1.0 / math.sqrt(length_x * NY * NZ)
    scale_out = 1.0 / math.sqrt(MX * MY * MZ * C)
    spectrum = analyse(fields, tables, offset) * scale_in
    slab_weight = lax.all_gather(spectral_weight, "batch", axis=3, tiled=True)
    mixed_modes = spectral_mix(spectrum, slab_weight)
    kernel_part = synthesise(mixed_modes, tables, offset, width_x) * scale_out
    linear = contract("bcxyz,co->boxyz", fields, local_weight)
    slope_grad = (cotangent.astype(jnp.float32) * gelu_slope(linear + kernel_part)).astype(
        jnp.bfloat16
    )
    grad_modes = analyse(slope_grad, tables, offset) * scale_out
    weight_part, back_modes = spectral_adjoint(grad_modes, spectrum, slab_weight)
    weight_grad = lax.psum_scatter(
        weight_part.astype(jnp.bfloat16), "batch", scatter_dimension=3, tiled=True
    ).astype(jnp.float32)
    through = contract("boxyz,co->bcxyz", slope_grad, local_weight)
    field_grad = (through + synthesise(back_modes, tables, offset, width_x) * scale_in).astype(
        jnp.bfloat16
    )
    return (field_grad, weight_grad)


def solution(mesh):
    placed = (
        P("batch", None, "slab", None, None),
        P("batch", None, "slab", None, None),
        P(),
        P(None, None, None, ("slab", "batch")),
    )
    return jax.shard_map(
        body,
        mesh=mesh,
        in_specs=placed,
        out_specs=(P("batch", None, "slab", None, None), P(None, None, None, ("slab", "batch"))),
        check_vma=False,
    )
```

profile of v0, /device:TPU:1, one launch (start us, length us, event | category | flops | bytes accessed | tf_op | source)
XLA Modules:
  0.0 629.3 jit_solution(2085436150373383262)
XLA Ops:
  8.2 0.2 cosine_convert_fusion.2
  8.4 0.2 fusion.106
  8.6 0.1 fusion.83
  8.7 0.1 copy.154
  8.8 2.9 convert_bitcast_fusion.1
  11.7 1.7 fusion.45
  13.4 1.7 copy.58
  15.2 0.5 copy.59
  15.7 2.9 convolution_bitcast_fusion.3
  18.6 10.4 %copy.60 = f32[1,32,2,512,32]{4,3,1,2,0:T(8,128)} copy(f32[1,32,2,512,32]{3,4,1,2,0:T(8,128)} %convolution_bitcast_fusion.3) | data formatting | bytes 8388608 | tf_op jit(solution)/shard_map/bcxpm,xpqk->bcqmk/transpose | solution.py:63
  29.0 13.0 %reshape.816 = f32[1,32,2,16384]{3,1,2,0:T(8,128)} reshape(f32[1,32,2,512,32]{4,3,1,2,0:T(8,128)} %copy.60) | data formatting | bytes 8388608 | tf_op jit(solution)/shard_map/reshape | solution.py:74
  42.1 1.0 copy-done.2
  43.1 2.4 copy.61
  45.5 139.3 %reduce-scatter.6.cloned.1.call-done = f32[1,32,2,256]{3,1,2,0:T(8,128)} async-done(((f32[1,32,2,16384]{3,1,2,0:T(8,128)}), f32[1,32,2,256]{3,1,2,0:T(8,128)}) %reduce-scatter.6.cloned.1.call-update) | async-done | bytes 65552 | tf_op jit(solution)/shard_map/reduce_scatter | solution.py:75
  184.8 0.8 broadcast_multiply_fusion.1
  185.7 0.1 copy.155
  185.8 0.1 copy.156
  185.9 6.7 %fusion.13 = (f32[256,32]{1,0:T(8,128)S(1)}, f32[256,32]{1,0:T(8,128)S(1)}, f32[256,32]{1,0:T(8,128)S(1)}, f32[256,32]{1,0:T(8,128)S(1)}) fusion(f32[256,32]{1,0:T(8,128)S(1)} %copy.156, bf16[2,32,32,256]{2,1,0,3:T(8,128)(2,1)} %all-gather.4.cloned.1.call-done, f32[256,32]{1,0:T(8,128)S(1)} %copy.155), kind=kLoop, calls=%fused_computation.26 | loop fusion | flops 2588672 | bytes 1245184
  192.8 0.1 copy.107
  192.9 0.1 copy.89
  193.0 0.6 pad_maximum_fusion.1
  193.7 0.3 reduce-scatter.8.cloned.1.call-start
  194.0 0.2 negate_convert_fusion.1
  194.2 0.1 fusion.84
  194.3 0.1 copy.153
  194.6 0.2 cosine_convert_fusion.3
  194.7 75.3 %all-gather.6.cloned.1.call-done = bf16[1,32,2,16384]{3,1,2,0:T(8,128)(2,1)} async-done(((bf16[1,32,2,256]{3,1,2,0:T(8,128)(2,1)}), bf16[1,32,2,16384]{3,1,2,0:T(8,128)(2,1)}) %all-gather.6.cloned.1.call-update) | async-done | bytes 2097168 | tf_op jit(solution)/shard_map/all_gather | solution.py:82
  270.1 9.4 %reshape.819 = bf16[32,2,512,32]{3,2,0,1:T(8,128)(2,1)} reshape(bf16[1,32,2,16384]{3,1,2,0:T(8,128)(2,1)} %all-gather.6.cloned.1.call-done) | data formatting | bytes 4194304 | tf_op jit(solution)/shard_map/reshape.27
  279.4 5.6 fusion.63
  285.1 0.5 copy.63
  285.6 2.0 copy.64
  287.6 5.2 convolution_bitcast_fusion.1
  292.8 18.6 %fusion.26 = bf16[32,4,128,128]{3,0,2,1:T(8,128)(2,1)S(1)} fusion(f32[128,32,4,128]{3,0,2,1:T(8,128)} %convolution_bitcast_fusion.1, bf16[1,32,4,128,128]{4,3,2,1,0:T(8,128)(2,1)} %param.5, bf16[32,4,128,128]{3,2,1,0:T(8,128)(2,1)} %bitcast.381, bf16[32,32]{1,0:T(8,128)(2,1)S(1)} %copy-done), kind=kOutput, calls=%fused_computation.41 | convolution fusion | flops 161480704 | bytes 20973568 | tf_op jit(solution)/shard_map/bcxyz,co->boxyz/dot_general | solution.py:63
  311.4 2.0 copy-done.1
  313.4 4.6 convert_bitcast_fusion
  318.0 1.7 fusion.48
  319.7 1.7 copy.69
  321.5 0.5 copy.70
  322.0 2.9 convolution_bitcast_fusion.2
  324.9 10.4 %copy.71 = f32[1,32,2,512,32]{4,3,1,2,0:T(8,128)} copy(f32[1,32,2,512,32]{3,4,1,2,0:T(8,128)} %convolution_bitcast_fusion.2) | data formatting | bytes 8388608 | tf_op jit(solution)/shard_map/bcxpm,xpqk->bcqmk/transpose | solution.py:63
  335.3 13.0 %reshape.825 = f32[1,32,2,16384]{3,1,2,0:T(8,128)} reshape(f32[1,32,2,512,32]{4,3,1,2,0:T(8,128)} %copy.71) | data formatting | bytes 8388608 | tf_op jit(solution)/shard_map/reshape | solution.py:74
  348.4 137.4 %reduce-scatter.8.cloned.1.call-done = f32[1,32,2,256]{3,1,2,0:T(8,128)} async-done(((f32[1,32,2,16384]{3,1,2,0:T(8,128)}), f32[1,32,2,256]{3,1,2,0:T(8,128)}) %reduce-scatter.8.cloned.1.call-update) | async-done | bytes 65552 | tf_op jit(solution)/shard_map/reduce_scatter | solution.py:75
  485.8 0.8 broadcast_multiply_fusion
  486.6 0.4 fusion.73
  487.0 0.1 pad_maximum_fusion
  487.1 6.7 %copy.151 = bf16[2,32,32,256]{2,1,0,3:T(8,128)(2,1)} copy(bf16[2,32,32,256]{3,2,1,0:T(8,128)(2,1)S(1)} %pad_maximum_fusion) | data formatting | bytes 2097152
  493.7 6.8 %reshape.875 = bf16[256,2048]{1,0:T(8,128)(2,1)} reshape(bf16[256,2,32,32]{3,2,1,0:T(8,128)(2,1)} %bitcast.379) | data formatting | bytes 2097152
  500.6 0.1 copy.157
  500.7 0.1 copy.158
  500.8 6.1 fusion.17
  507.1 0.1 copy.141
  507.3 0.6 pad_maximum_fusion.2
  507.9 20.5 %reduce-scatter.10.cloned.1.call-done = bf16[64,2048]{1,0:T(8,128)(2,1)} async-done(((bf16[256,2048]{1,0:T(8,128)(2,1)}), bf16[64,2048]{1,0:T(8,128)(2,1)}) %reduce-scatter.10.cloned.1.call-update) | async-done | bytes 262160
  528.4 1.9 reshape.876
  530.3 1.2 copy.152
  531.5 1.1 convert_element_type.277
  532.6 51.8 %all-gather.8.cloned.1.call-done = bf16[1,32,2,16384]{3,1,2,0:T(8,128)(2,1)} async-done(((bf16[1,32,2,256]{3,1,2,0:T(8,128)(2,1)}), bf16[1,32,2,16384]{3,1,2,0:T(8,128)(2,1)}) %all-gather.8.cloned.1.call-update) | async-done | bytes 2097168 | tf_op jit(solution)/shard_map/all_gather | solution.py:82
  584.3 9.4 %reshape.828 = bf16[32,2,512,32]{3,2,0,1:T(8,128)(2,1)} reshape(bf16[1,32,2,16384]{3,1,2,0:T(8,128)(2,1)} %all-gather.8.cloned.1.call-done) | data formatting | bytes 4194304 | tf_op jit(solution)/shard_map/reshape.50
  593.7 5.6 fusion.66
  599.4 0.5 copy.73
  599.9 2.3 copy.74
  602.2 5.2 convolution_bitcast_fusion
  607.3 10.7 %fusion.6 = bf16[1,32,4,128,128]{4,1,3,2,0:T(8,128)(2,1)S(1)} fusion(f32[128,32,4,128]{3,0,2,1:T(8,128)} %convolution_bitcast_fusion, bf16[32,4,128,128]{3,0,2,1:T(8,128)(2,1)} %copy-done.1, bf16[32,32]{1,0:T(8,128)(2,1)S(1)} %copy-done), kind=kOutput, calls=%fused_computation.8 | convolution fusion | flops 140509184 | bytes 16779264 | tf_op jit(solution)/shard_map/boxyz,co->bcxyz/dot_general | solution.py:63
  618.1 3.6 copy.77
  (36 shorter events, 1.0 us)
Async XLA Ops:
  8.0 284.8 %copy-start = (bf16[32,32]{1,0:T(8,128)(2,1)S(1)}, bf16[32,32]{1,0:T(8,128)(2,1)}, u32[]{:S(2)}) copy-start(bf16[32,32]{1,0:T(8,128)(2,1)} %param.6) | copy-start | bytes 6148
  8.0 176.8 %reduce-scatter.6.cloned.1.call-start = ((), (), s32[]{:S(2)}) async-start(), calls=%async_computation.3 | async-start | bytes 4259840 | tf_op jit(solution)/shard_map/reduce_scatter | solution.py:75
  42.0 1.0 copy-start.2
  42.0 143.9 %all-gather.4.cloned.1.call-start = ((), (), s32[]{:S(2)}) async-start(), calls=%async_computation.4 | async-start | bytes 5242880 | tf_op jit(solution)/shard_map/all_gather | solution.py:134
  45.5 224.6 %all-gather.6.cloned.1.call-start = ((), (), s32[]{:S(2)}) async-start(), calls=%async_computation.5 | async-start | bytes 2129920 | tf_op jit(solution)/shard_map/all_gather | solution.py:82
  193.7 292.1 %reduce-scatter.8.cloned.1.call-start = ((), (), s32[]{:S(2)}) async-start(), calls=%async_computation.6 | async-start | bytes 4259840 | tf_op jit(solution)/shard_map/reduce_scatter | solution.py:75
  311.4 2.0 copy-start.1
  348.3 180.1 %reduce-scatter.10.cloned.1.call-start = ((), (), s32[]{:S(2)}) async-start(), calls=%async_computation.8 | async-start | bytes 1310720
  500.6 83.7 %all-gather.8.cloned.1.call-start = ((), (), s32[]{:S(2)}) async-start(), calls=%async_computation.7 | async-start | bytes 2129920 | tf_op jit(solution)/shard_map/all_gather | solution.py:82
Sparse Core Ops, SparseCore 0:
  42.2 142.6 reduce-scatter.5
  193.8 76.2 all-gather.5
  348.5 137.2 reduce-scatter.7
  508.1 76.2 all-gather.7
Sparse Core Ops, SparseCore 1:
  45.6 54.3 all-gather.3
  500.7 27.7 reduce-scatter.9
where the time goes:
time: 637 us; the launch traced here: 629 us
  waiting for transfers between devices  424 us (67%)
  local copies, waits for them, and re-layouts  102 us (16%)
  matrix products  67.7 us (11%)
  other arithmetic  18.6 us (3%)
  between operations  15.9 us (2%)
    reduce_scatter x2, waiting for transfers between devices, analyse(): lax.psum_scatter(partial_sum, 'slab', scatter_dimension=3, tiled=True)  277 us
    all_gather x2, waiting for transfers between devices, synthesise(): whole = lax.all_gather(modes_part, 'slab', axis=3, tiled=True)  127 us
    dot_general x12, matrix products, contract(): return jnp.einsum(formula, left, right, preferred_element_type=jnp.float32)  67.7 us
    unnamed x20, local copies, waits for them, and re-layouts  26.1 us
    reshape x2, local copies, waits for them, and re-layouts, analyse(): partial_sum = partial_sum.reshape(samples, channels, 2, MY * MZ * MX)  26 us
    another operation x6, local copies, waits for them, and re-layouts  24.2 us
    transpose x2, local copies, waits for them, and re-layouts, contract(): return jnp.einsum(formula, left, right, preferred_element_type=jnp.float32)  20.9 us
    unnamed x7, waiting for transfers between devices  20.6 us
  transfers between devices with their start and end apart: 6, of which 5 were waited for; matrix products, arithmetic and copies ran while one was open for 2% of the time, Pallas kernels for 0%

commit v1 on v0

--- a/solution.py
+++ b/solution.py
@@ -4,6 +4,8 @@
 import jax
 import jax.numpy as jnp
 from jax import lax
+from jax.experimental import pallas as pl
+from jax.experimental.pallas import tpu as pltpu
 from jax.sharding import PartitionSpec as P
 
 C = 32
@@ -12,6 +14,7 @@
 MX = 32
 MY = 32
 MZ = 16
+MESH = pl.DeviceIdType.MESH
 
 
 def frequencies(number, signed):
@@ -63,27 +66,84 @@
     return jnp.einsum(formula, left, right, preferred_element_type=jnp.float32)
 
 
-def analyse(field, tables, offset):
+def exchange_kernel(slabs, batches, src, dst, send_sem, recv_sem, own_sem):
+    count = slabs * batches
+    me = lax.axis_index("slab") * batches + lax.axis_index("batch")
+
+    def place(index):
+        return (index // batches, index % batches)
+
+    barrier = pltpu.get_barrier_semaphore()
+
+    def greet(step, carry):
+        pl.semaphore_signal(
+            barrier, inc=1, device_id=place((me + step) % count), device_id_type=MESH
+        )
+        return carry
+
+    lax.fori_loop(1, count, greet, 0)
+    pl.semaphore_wait(barrier, count - 1)
+
+    def send(step, carry):
+        target = (me + step) % count
+        pltpu.make_async_remote_copy(
+            src_ref=src.at[target],
+            dst_ref=dst.at[me],
+            send_sem=send_sem,
+            recv_sem=recv_sem,
+            device_id=place(target),
+            device_id_type=MESH,
+        ).start()
+        return carry
+
+    lax.fori_loop(1, count, send, 0)
+    own = pltpu.make_async_copy(src.at[me], dst.at[me], own_sem)
+    own.start()
+    own.wait()
+    some = pl.ds(0, count - 1)
+    pltpu.make_async_copy(src.at[some], dst.at[some], send_sem).wait()
+    pltpu.make_async_copy(src.at[some], dst.at[some], recv_sem).wait()
+
+
+def exchange(messages):
+    slabs, batches = lax.axis_size("slab"), lax.axis_size("batch")
+    return pl.pallas_call(
+        partial(exchange_kernel, slabs, batches),
+        out_shape=jax.ShapeDtypeStruct(messages.shape, messages.dtype),
+        in_specs=[pl.BlockSpec(memory_space=pltpu.VMEM)],
+        out_specs=pl.BlockSpec(memory_space=pltpu.VMEM),
+        scratch_shapes=[pltpu.SemaphoreType.DMA] * 3,
+        compiler_params=pltpu.CompilerParams(collective_id=0, has_side_effects=True),
+    )(messages)
+
+
+def analyse(field, tables):
     analysis_y, pair_z, pair_x = (tables[0], tables[1], tables[2])
     first = contract("bcxyz,ypk->bcxpkz", field, analysis_y).astype(jnp.bfloat16)
     second = contract("bcxpyz,zpqk->bcxqyk", first, pair_z).astype(jnp.bfloat16)
-    samples, channels, width_x = (second.shape[0], second.shape[1], second.shape[2])
-    second = second.reshape(samples, channels, width_x, 2, MY * MZ)
-    rows = lax.dynamic_slice_in_dim(pair_x, offset, width_x, 0)
-    partial_sum = contract("bcxpm,xpqk->bcqmk", second, rows)
-    partial_sum = partial_sum.reshape(samples, channels, 2, MY * MZ * MX)
-    result = lax.psum_scatter(partial_sum, "slab", scatter_dimension=3, tiled=True)
-    return result
-
-
-def synthesise(modes_part, tables, offset, width_x):
+    channels, width_x = second.shape[1], second.shape[2]
+    slabs, batches = lax.axis_size("slab"), lax.axis_size("batch")
+    devices = slabs * batches
+    held = MY * MZ // devices
+    second = second.reshape(channels, width_x, 2, devices, held)
+    messages = jnp.transpose(second, (3, 1, 2, 4, 0)).reshape(devices, width_x, 2 * held * channels)
+    got = exchange(messages).reshape(slabs, batches, width_x, 2, held, channels)
+    table = pair_x.reshape(slabs, width_x, 2, 2, MX)
+    return contract("wsxpbc,wxpqk->scqbk", got, table).reshape(batches, channels, 2, held * MX)
+
+
+def synthesise(modes_part, tables, width_x):
     back_x, back_z, final_y = (tables[3], tables[4], tables[5])
     samples, channels = (modes_part.shape[0], modes_part.shape[1])
-    whole = lax.all_gather(modes_part, "slab", axis=3, tiled=True)
-    grid = whole.reshape(samples, channels, 2, MY * MZ, MX)
-    columns = lax.dynamic_slice_in_dim(back_x, offset, width_x, 3)
-    first = contract("bcpmk,kpqx->bcxqm", grid, columns).astype(jnp.bfloat16)
-    first = first.reshape(samples, channels, width_x, 2, MY, MZ)
+    slabs, batches = lax.axis_size("slab"), lax.axis_size("batch")
+    devices = slabs * batches
+    held = MY * MZ // devices
+    grid = modes_part.reshape(samples, channels, 2, held, MX)
+    columns = back_x.reshape(MX, 2, 2, slabs, width_x)
+    first = contract("scpbk,kpqwx->wsxqbc", grid, columns).astype(jnp.bfloat16)
+    messages = first.reshape(devices, width_x, 2 * held * channels)
+    got = exchange(messages).reshape(MY, MZ // held, width_x, 2, held, channels)
+    first = jnp.transpose(got, (5, 2, 3, 0, 1, 4)).reshape(1, channels, width_x, 2, MY, MZ)
     second = contract("bcxpyk,kpqz->bcxqyz", first, back_z).astype(jnp.bfloat16)
     return contract("bcxpkz,pky->bcxyz", second, final_y)
 
@@ -127,24 +187,19 @@
     width_x = fields.shape[2]
     length_x = width_x * lax.axis_size("slab")
     tables = make_tables(length_x)
-    offset = lax.axis_index("slab") * width_x
     scale_in = 1.0 / math.sqrt(length_x * NY * NZ)
     scale_out = 1.0 / math.sqrt(MX * MY * MZ * C)
-    spectrum = analyse(fields, tables, offset) * scale_in
-    slab_weight = lax.all_gather(spectral_weight, "batch", axis=3, tiled=True)
-    mixed_modes = spectral_mix(spectrum, slab_weight)
-    kernel_part = synthesise(mixed_modes, tables, offset, width_x) * scale_out
+    spectrum = analyse(fields, tables) * scale_in
+    mixed_modes = spectral_mix(spectrum, spectral_weight)
+    kernel_part = synthesise(mixed_modes, tables, width_x) * scale_out
     linear = contract("bcxyz,co->boxyz", fields, local_weight)
     slope_grad = (cotangent.astype(jnp.float32) * gelu_slope(linear + kernel_part)).astype(
         jnp.bfloat16
     )
-    grad_modes = analyse(slope_grad, tables, offset) * scale_out
-    weight_part, back_modes = spectral_adjoint(grad_modes, spectrum, slab_weight)
-    weight_grad = lax.psum_scatter(
-        weight_part.astype(jnp.bfloat16), "batch", scatter_dimension=3, tiled=True
-    ).astype(jnp.float32)
+    grad_modes = analyse(slope_grad, tables) * scale_out
+    weight_grad, back_modes = spectral_adjoint(grad_modes, spectrum, spectral_weight)
     through = contract("boxyz,co->bcxyz", slope_grad, local_weight)
-    field_grad = (through + synthesise(back_modes, tables, offset, width_x) * scale_in).astype(
+    field_grad = (through + synthesise(back_modes, tables, width_x) * scale_in).astype(
         jnp.bfloat16
     )
     return (field_grad, weight_grad)

time: 637 us -> 206 us (0.32)
  waiting for transfers between devices: 424 us -> 0 us
  Pallas kernels: 0 us -> 92.6 us
  local copies, waits for them, and re-layouts: 102 us -> 40.1 us
  other arithmetic: 18.6 us -> 1.51 us
  between operations: 15.9 us -> 1.24 us
    reduce_scatter x2 -> x0, waiting for transfers between devices: 277 us -> none  [analyse(): lax.psum_scatter(partial_sum, 'slab', scatter_dimension=3, tiled=True)]
    all_gather x3 -> x0, waiting for transfers between devices: 127 us -> none  [the longest x2 127 us: synthesise(): whole = lax.all_gather(modes_part, 'slab', axis=3, tiled=True)]
    pallas_call x0 -> x4, Pallas kernels: none -> 92.6 us  [exchange(): pl.pallas_call(partial(exchange_kernel, slabs, batches), out_shape=jax.Sh...]
    another operation x6 -> x4, local copies, waits for them, and re-layouts: 24.2 us -> 0.45 us  [the longest x2 0.23 us: spectral_adjoint(): jnp.stack([back_real, back_imag], 2).astype(jnp.bfloat16)]
    unnamed x7 -> x0, waiting for transfers between devices: 20.6 us -> none
    unnamed x20 -> x16, local copies, waits for them, and re-layouts: 26.1 us -> 9.35 us
    transpose x2 -> x4, local copies, waits for them, and re-layouts: 20.9 us -> 5.27 us  [the longest x2 4.15 us: synthesise(): jnp.transpose(got, (5, 2, 3, 0, 1, 4))]
    dot_general x12, matrix products: 67.7 us -> 53.9 us  [contract(): return jnp.einsum(formula, left, right, preferred_element_type=jnp.float32)]
  transfers between devices with their start and end apart: 6 -> 0, of which waited for: 5 -> 0; matrix products, arithmetic and copies ran while one was open for 2% -> 0% of each run, Pallas kernels for 0% -> 0%
where the time goes in v1:
time: 206 us; the launch traced here: 203 us
  Pallas kernels  92.6 us (45%)
  matrix products  67.3 us (33%)
  local copies, waits for them, and re-layouts  40.1 us (19%)
    pallas_call x4, Pallas kernels, exchange(): pl.pallas_call(partial(exchange_kernel, slabs, batches), out_shape=jax.Sh...  92.6 us
    dot_general x12, matrix products, contract(): return jnp.einsum(formula, left, right, preferred_element_type=jnp.float32)  53.9 us
    unnamed x16, local copies, waits for them, and re-layouts  9.35 us
    reshape x4, local copies, waits for them, and re-layouts, analyse(): got = exchange(messages).reshape(slabs, batches, width_x, 2, held, channels)  8.2 us
    reshape x2, local copies, waits for them, and re-layouts, synthesise(): got = exchange(messages).reshape(MY, MZ // held, width_x, 2, held, channels)  5.8 us
    reshape x4, local copies, waits for them, and re-layouts, synthesise(): messages = first.reshape(devices, width_x, 2 * held * channels)  4.52 us
    transpose x2, local copies, waits for them, and re-layouts, synthesise(): jnp.transpose(got, (5, 2, 3, 0, 1, 4))  4.15 us

profile of v1, /device:TPU:1, one launch (start us, length us, event | category | flops | bytes accessed | tf_op | source)
XLA Modules:
  0.0 202.7 jit_solution(7355235893792441820)
XLA Ops:
  0.6 1.1 fusion.125
  1.7 0.8 copy.106
  2.5 0.2 cosine_convert_fusion.2
  2.7 2.9 %convert_bitcast_fusion.1 = bf16[32,4,2,32,128]{4,3,1,0,2:T(8,128)(2,1)S(1)} fusion(bf16[1,32,4,128,128]{4,3,2,1,0:T(8,128)(2,1)} %param.4, bf16[128,1,32]{0,2,1:T(8,128)(2,1)S(1)} %get-tuple-element.25, bf16[128,1,32]{0,2,1:T(8,128)(2,1)S(1)} %get-tuple-element.24), kind=kOutput, calls=%fused_computation.36 | convolution fusion | flops 269516800 | bytes 6307840 | tf_op jit(solution)/shard_map/bcxyz,ypk->bcxpkz/dot_general | solution.py:66
  5.6 0.1 negate_convert_fusion.4
  5.6 0.1 fusion.110
  5.7 1.7 fusion.33
  7.4 1.9 copy.42
  9.3 0.6 copy.43
  9.9 0.9 copy.44.src
  10.8 26.1 %shard_map.59 = bf16[256,4,128]{2,1,0:T(4,128)(2,1)} custom-call(bf16[256,4,128]{2,1,0:T(4,128)(2,1)} %copy.44.src), custom_call_target="tpu_custom_call" | custom-call | tf_op jit(solution)/shard_map/pallas_call | solution.py:110
  36.9 2.9 %reshape.717 = bf16[64,4,4,2,2,32]{5,4,3,2,1,0:T(2,128)(2,1)S(1)} reshape(bf16[256,4,128]{2,1,0:T(4,128)(2,1)} %shard_map.59) | data formatting | bytes 524288 | tf_op jit(solution)/shard_map/reshape | solution.py:130
  39.8 1.2 copy.46
  41.0 0.3 negate_convert_fusion
  41.4 0.5 fusion.46
  42.0 0.5 fusion.60
  42.6 0.8 copy.108
  43.4 0.5 fusion.48
  43.9 0.1 copy.52
  44.0 0.5 fusion.62
  44.6 0.5 fusion.47
  45.1 0.1 copy.51
  45.2 0.3 fusion.80
  45.6 0.3 fusion.44
  45.9 1.0 copy.99
  47.0 1.2 reshape.718.src
  48.2 22.5 %shard_map.60 = bf16[256,4,128]{2,1,0:T(4,128)(2,1)} custom-call(bf16[256,4,128]{2,1,0:T(4,128)(2,1)} %reshape.718.src), custom_call_target="tpu_custom_call" | custom-call | tf_op jit(solution)/shard_map/pallas_call | solution.py:110
  70.7 2.9 %reshape.677 = bf16[32,8,4,2,2,32]{5,4,3,2,1,0:T(2,128)(2,1)S(1)} reshape(bf16[256,4,128]{2,1,0:T(4,128)(2,1)} %shard_map.60) | data formatting | bytes 524288 | tf_op jit(solution)/shard_map/reshape | solution.py:145
  73.7 2.1 %copy.55 = bf16[32,4,2,32,8,2]{3,5,4,2,1,0:T(2,128)(2,1)S(1)} copy(bf16[32,4,2,32,8,2]{0,5,2,1,4,3:T(2,128)(2,1)S(1)} %bitcast.318) | data formatting | bytes 524288 | tf_op jit(solution)/shard_map/transpose | solution.py:146
  75.8 0.1 negate_convert_fusion.5
  75.9 0.2 cosine_convert_fusion.3
  76.1 5.2 %convolution_bitcast_fusion.1 = f32[128,32,4,128]{3,0,2,1:T(8,128)} fusion(bf16[32,4,2,32,16,1]{3,4,2,1,0,5:T(8,128)(2,1)S(1)} %bitcast.314, bf16[16,1,2,128]{3,0,1,2:T(8,128)(2,1)S(1)} %get-tuple-element.13, bf16[16,1,2,128]{3,0,1,2:T(8,128)(2,1)S(1)} %get-tuple-element.12, bf16[1,32,128]{2,1,0:T(8,128)(2,1)S(1)} %get-tuple-element.23, ...), kind=kOutput, calls=%fused_computation.23 | convolution fusion | flops 336658432 | bytes 8683520 | tf_op jit(solution)/shard_map/bcxpkz,pky->bcxyz/dot_general | solution.py:66
  81.3 18.4 %fusion.14 = bf16[32,4,128,128]{3,0,2,1:T(8,128)(2,1)S(1)} fusion(f32[128,32,4,128]{3,0,2,1:T(8,128)} %convolution_bitcast_fusion.1, bf16[1,32,4,128,128]{4,3,2,1,0:T(8,128)(2,1)} %param.5, bf16[32,4,128,128]{3,2,1,0:T(8,128)(2,1)} %bitcast.316, bf16[32,32]{1,0:T(8,128)(2,1)S(1)} %copy-done), kind=kOutput, calls=%fused_computation.21 | convolution fusion | flops 161480704 | bytes 20973568 | tf_op jit(solution)/shard_map/bcxyz,co->boxyz/dot_general | solution.py:66
  99.7 2.0 copy-done.1
  101.7 4.6 %convert_bitcast_fusion = bf16[32,4,2,32,128]{4,3,1,0,2:T(8,128)(2,1)S(1)} fusion(bf16[32,4,128,128]{3,0,2,1:T(8,128)(2,1)S(1)} %fusion.14, bf16[128,1,32]{0,2,1:T(8,128)(2,1)S(1)} %get-tuple-element.25, bf16[128,1,32]{0,2,1:T(8,128)(2,1)S(1)} %get-tuple-element.24), kind=kOutput, calls=%fused_computation.35 | convolution fusion | flops 269516800 | bytes 6307840 | tf_op jit(solution)/shard_map/bcxyz,ypk->bcxpkz/dot_general | solution.py:66
  106.3 1.7 fusion.36
  108.0 1.7 copy.60
  109.7 0.6 copy.61
  110.3 0.9 copy.62.src
  111.2 22.0 %shard_map.61 = bf16[256,4,128]{2,1,0:T(4,128)(2,1)} custom-call(bf16[256,4,128]{2,1,0:T(4,128)(2,1)} %copy.62.src), custom_call_target="tpu_custom_call" | custom-call | tf_op jit(solution)/shard_map/pallas_call | solution.py:110
  133.2 2.9 %reshape.719 = bf16[64,4,4,2,2,32]{5,4,3,2,1,0:T(2,128)(2,1)S(1)} reshape(bf16[256,4,128]{2,1,0:T(4,128)(2,1)} %shard_map.61) | data formatting | bytes 524288 | tf_op jit(solution)/shard_map/reshape | solution.py:130
  136.1 1.2 copy.64
  137.3 1.4 fusion.45
  138.7 0.9 fusion.56
  139.6 0.9 fusion.50
  140.6 0.1 copy.68
  140.7 0.9 fusion.58
  141.6 0.9 fusion.49
  142.5 0.1 copy.67
  142.7 1.2 fusion.43
  143.8 1.0 copy.102
  144.9 1.2 reshape.720.src
  146.1 22.0 %shard_map.62 = bf16[256,4,128]{2,1,0:T(4,128)(2,1)} custom-call(bf16[256,4,128]{2,1,0:T(4,128)(2,1)} %reshape.720.src), custom_call_target="tpu_custom_call" | custom-call | tf_op jit(solution)/shard_map/pallas_call | solution.py:110
  168.1 2.9 %reshape.686 = bf16[32,8,4,2,2,32]{5,4,3,2,1,0:T(2,128)(2,1)S(1)} reshape(bf16[256,4,128]{2,1,0:T(4,128)(2,1)} %shard_map.62) | data formatting | bytes 524288 | tf_op jit(solution)/shard_map/reshape | solution.py:145
  171.0 2.0 %copy.71 = bf16[32,4,2,32,8,2]{3,5,4,2,1,0:T(2,128)(2,1)S(1)} copy(bf16[32,4,2,32,8,2]{0,5,2,1,4,3:T(2,128)(2,1)S(1)} %bitcast.320) | data formatting | bytes 524288 | tf_op jit(solution)/shard_map/transpose | solution.py:146
  173.0 5.2 %convolution_bitcast_fusion = f32[128,32,4,128]{3,0,2,1:T(8,128)} fusion(bf16[32,4,2,32,16,1]{3,4,2,1,0,5:T(8,128)(2,1)S(1)} %bitcast.315, bf16[16,1,2,128]{3,0,1,2:T(8,128)(2,1)S(1)} %get-tuple-element.13, bf16[16,1,2,128]{3,0,1,2:T(8,128)(2,1)S(1)} %get-tuple-element.12, bf16[1,32,128]{2,1,0:T(8,128)(2,1)S(1)} %get-tuple-element.23, ...), kind=kOutput, calls=%fused_computation.22 | convolution fusion | flops 336658432 | bytes 8683520 | tf_op jit(solution)/shard_map/bcxpkz,pky->bcxyz/dot_general | solution.py:66
  178.2 10.7 %fusion.6 = bf16[1,32,4,128,128]{4,1,3,2,0:T(8,128)(2,1)S(1)} fusion(f32[128,32,4,128]{3,0,2,1:T(8,128)} %convolution_bitcast_fusion, bf16[32,4,128,128]{3,0,2,1:T(8,128)(2,1)} %copy-done.1, bf16[32,32]{1,0:T(8,128)(2,1)S(1)} %copy-done), kind=kOutput, calls=%fused_computation.8 | convolution fusion | flops 140509184 | bytes 16779264 | tf_op jit(solution)/shard_map/boxyz,co->bcxyz/dot_general | solution.py:66
  189.0 3.6 %copy.74 = bf16[1,32,4,128,128]{4,3,2,1,0:T(8,128)(2,1)} copy(bf16[1,32,4,128,128]{4,1,3,2,0:T(8,128)(2,1)S(1)} %fusion.6) | data formatting | bytes 8388608
  192.6 1.8 fusion.69
  194.4 2.1 %fusion.39 = f32[1,32,32,64]{2,1,3,0:T(8,128)S(1)} fusion(f32[64,32,32]{2,1,0:T(8,128)S(1)} %fusion.69, f32[4,32,1,64]{1,3,0,2:T(8,128)S(1)} %get-tuple-element.11, f32[4,32,1,64]{1,3,0,2:T(8,128)S(1)} %get-tuple-element.8), kind=kOutput, calls=%fused_computation.40 | convolution fusion | flops 3211264 | bytes 589824 | tf_op jit(solution)/shard_map/sok,sck->cok/dot_general | solution.py:171
  196.5 1.8 fusion.70
  198.3 1.9 fusion.40
  200.2 0.2 pad_maximum_fusion
  200.4 2.1 %copy.75 = f32[2,32,32,64]{3,2,1,0:T(8,128)} copy(f32[2,32,32,64]{2,1,3,0:T(8,128)S(1)} %pad_maximum_fusion) | data formatting | bytes 1048576
  (18 shorter events, 0.2 us)
Async XLA Ops:
  0.6 80.6 %copy-start = (bf16[32,32]{1,0:T(8,128)(2,1)S(1)}, bf16[32,32]{1,0:T(8,128)(2,1)}, u32[]{:S(2)}) copy-start(bf16[32,32]{1,0:T(8,128)(2,1)} %param.6) | copy-start | bytes 6148
  41.4 0.6 copy-start.2
  45.6 2.6 %copy-start.3 = (bf16[32,1,1,64,4]{3,0,1,4,2:T(8,128)(2,1)}, bf16[32,1,1,64,4]{3,0,1,4,2:T(8,128)(2,1)S(1)}, u32[]{:S(2)}) copy-start(bf16[32,1,1,64,4]{3,0,1,4,2:T(8,128)(2,1)S(1)} %get-tuple-element.16) | copy-start | bytes 49156
  45.6 2.6 %copy-start.4 = (bf16[32,1,1,64,4]{3,0,1,4,2:T(8,128)(2,1)}, bf16[32,1,1,64,4]{3,0,1,4,2:T(8,128)(2,1)S(1)}, u32[]{:S(2)}) copy-start(bf16[32,1,1,64,4]{3,0,1,4,2:T(8,128)(2,1)S(1)} %get-tuple-element.17) | copy-start | bytes 49156
  45.6 2.6 %copy-start.5 = (bf16[32,1,1,64,4]{3,0,1,4,2:T(8,128)(2,1)}, bf16[32,1,1,64,4]{3,0,1,4,2:T(8,128)(2,1)S(1)}, u32[]{:S(2)}) copy-start(bf16[32,1,1,64,4]{3,0,1,4,2:T(8,128)(2,1)S(1)} %get-tuple-element.18) | copy-start | bytes 49156
  99.6 2.0 copy-start.1

commit v2 on v0

v2 whole, which is shorter than its diff:
```python
from functools import partial
import math

import jax
import jax.numpy as jnp
import ml_dtypes
import numpy as np
from jax import lax
from jax.experimental import pallas as pl
from jax.experimental.pallas import tpu as pltpu
from jax.sharding import PartitionSpec as P

C = 32
NX = 256
NY = 128
NZ = 128
MX = 32
MY = 32
MZ = 16
SLABS = 64
BATCHES = 4
DEVICES = SLABS * BATCHES
WIDTH = NX // SLABS
HELD = MY * MZ // DEVICES
HIGH = MZ // HELD
GROUP = 8
GROUPS = C // GROUP
BAND = 16
MESH = pl.DeviceIdType.MESH
F32 = jnp.float32
BF16 = jnp.bfloat16
SCALE_IN = 1.0 / math.sqrt(NX * NY * NZ)
SCALE_OUT = 1.0 / math.sqrt(MX * MY * MZ * C)


def wave_table(number, length, signed):
    numbers = np.arange(number)
    if signed:
        numbers = np.where(numbers < number // 2, numbers, numbers - number)
    phases = np.mod(numbers[:, None] * np.arange(length)[None, :], length).astype(np.float32)
    angles = phases * np.float32(2.0 * math.pi / length)
    return (np.cos(angles).astype(np.float32), np.sin(angles).astype(np.float32))


def make_tables():
    cos_y, sin_y = wave_table(MY, NY, True)
    cos_z, sin_z = wave_table(MZ, NZ, False)
    cos_x, sin_x = wave_table(MX, NX, True)
    eye = np.eye(GROUP, dtype=np.float32)
    pair_y = np.stack([cos_y, -sin_y])
    analysis_y = np.einsum("pky,ab->pkaby", pair_y, eye).reshape(2 * MY * GROUP, GROUP * NY)
    synthesis_y = np.einsum("pky,ab->aypkb", pair_y, eye).reshape(GROUP * NY, 2 * MY * GROUP)
    analysis_z = np.stack([np.stack([cos_z, sin_z], 1), np.stack([-sin_z, cos_z], 1)])
    analysis_z = analysis_z.reshape(2, HIGH, HELD, 2 * NZ).transpose(1, 0, 2, 3).reshape(2 * MZ, 2 * NZ)
    synthesis_z = np.stack([np.stack([cos_z, sin_z], 1), np.stack([-sin_z, cos_z], 1)])
    synthesis_z = synthesis_z.reshape(2, HIGH, HELD, 2 * NZ).transpose(1, 0, 2, 3).reshape(2 * MZ, 2 * NZ)
    both_x = np.stack([cos_x, sin_x]).reshape(2, MX, SLABS, WIDTH).transpose(0, 1, 3, 2)
    analysis_x = both_x.reshape(2 * MX, WIDTH * SLABS)
    synthesis_x = both_x.transpose(3, 2, 0, 1).reshape(SLABS, WIDTH * 2 * MX)
    tables = (analysis_y, synthesis_y, analysis_z, synthesis_z, analysis_x, synthesis_x)
    return tuple(np.ascontiguousarray(table).astype(ml_dtypes.bfloat16) for table in tables)


def matmul(left, right):
    return jnp.dot(left, right, preferred_element_type=F32)


def gelu_slope(values):
    size = jnp.abs(values)
    inverse = 1.0 / (1.0 + (0.3275911 / math.sqrt(2.0)) * size)
    tail = 0.5 * 1.061405429 * inverse - 0.5 * 1.453152027
    tail = tail * inverse + 0.5 * 1.421413741
    tail = tail * inverse - 0.5 * 0.284496736
    tail = tail * inverse + 0.5 * 0.254829592
    tail = tail * inverse - size * (1.0 / math.sqrt(2.0 * math.pi))
    below = jnp.exp(-0.5 * values * values) * tail
    return jnp.where(values >= 0.0, 1.0 - below, below)


def lane_groups(value):
    lanes = lax.broadcasted_iota(jnp.int32, value.shape, 1) // C
    return [jnp.where(lanes == group, value, 0.0) for group in range(WIDTH)]


def spread(weight):
    rows = C * BAND
    left = (
        lax.broadcasted_iota(jnp.int32, (rows, C), 0) // BAND
        == lax.broadcasted_iota(jnp.int32, (rows, C), 1)
    ).astype(F32).astype(BF16)
    right = (
        lax.broadcasted_iota(jnp.int32, (C, rows), 1) // BAND
        == lax.broadcasted_iota(jnp.int32, (C, rows), 0)
    ).astype(F32).astype(BF16)
    whole = matmul(matmul(left, weight).astype(BF16), right)
    same = (
        lax.broadcasted_iota(jnp.int32, (rows, rows), 0) % BAND
        == lax.broadcasted_iota(jnp.int32, (rows, rows), 1) % BAND
    )
    return jnp.where(same, whole, 0.0).astype(BF16)


def kernel(
    fields, cotangent, forward_map, backward_map, weights,
    analysis_y, synthesis_y, analysis_z, synthesis_z, analysis_x, synthesis_x,
    field_grad, weight_grad,
    sent, got, grid, flat, linear, slope, doubled, values, grads, modes, result, spread_map,
    send_sem, recv_sem, own_sem,
):
    me = lax.axis_index("slab") * BATCHES + lax.axis_index("batch")

    def place(index):
        return (index // BATCHES, index % BATCHES)

    barrier = pltpu.get_barrier_semaphore()

    def greet(step, carry):
        pl.semaphore_signal(
            barrier, inc=1, device_id=place((me + step) % DEVICES), device_id_type=MESH
        )
        return carry

    lax.fori_loop(1, DEVICES, greet, 0)

    def send(turn, target):
        @pl.when(target != me)
        def _():
            pltpu.make_async_remote_copy(
                src_ref=sent.at[turn, target],
                dst_ref=got.at[turn, me],
                send_sem=send_sem.at[turn],
                recv_sem=recv_sem.at[turn],
                device_id=place(target),
                device_id_type=MESH,
            ).start()

        @pl.when(target == me)
        def _():
            pltpu.make_async_copy(
                sent.at[turn, me], got.at[turn, me], own_sem.at[turn]
            ).start()

    def receive(turn):
        pltpu.make_async_copy(sent.at[turn, me], got.at[turn, me], own_sem.at[turn]).wait()
        some = pl.ds(0, DEVICES - 1)
        pltpu.make_async_copy(
            sent.at[turn, some], got.at[turn, some], recv_sem.at[turn]
        ).wait()

        def unpack(step, carry):
            for inner in range(8):
                index = step * 8 + inner
                flat[pl.ds(pl.multiple_of(index * 4, 4), 4), :] = got[turn, index].astype(F32)
            return carry

        lax.fori_loop(0, DEVICES // 8, unpack, 0)

    def analyse_y(source):
        def step(index, carry):
            pair = (index // GROUPS) * 2
            group = index % GROUPS
            channels = pl.ds(group * GROUP, GROUP)
            planes = [
                source[channels, pair + inner].reshape(GROUP * NY, NZ) for inner in range(2)
            ]
            first = matmul(analysis_y[...], jnp.concatenate(planes, 1))
            first = first.reshape(2, MY, GROUP, 2 * NZ)
            for inner in range(2):
                row = pl.multiple_of((pair + inner) * C + group * GROUP, GROUP)
                for part in range(2):
                    grid[:, pl.ds(row, GROUP), part * NZ:(part + 1) * NZ] = first[
                        part, :, :, inner * NZ:(inner + 1) * NZ
                    ]
            return carry

        lax.fori_loop(0, 2 * GROUPS, step, 0)

    def analyse_z(turn):
        def step(index, carry):
            ky = (me // HIGH + index) % MY
            first = grid[ky].astype(BF16)
            second = lax.dot_general(
                analysis_z[...], first, (((1,), (1,)), ((), ())), preferred_element_type=F32
            )
            for high in range(HIGH):
                target = ky * HIGH + high
                sent[turn, target] = second[4 * high:4 * high + 4].astype(BF16)
                send(turn, target)
            return carry

        lax.fori_loop(0, MY, step, 0)

    def analyse_x(target, scale):
        for sample in range(BATCHES):
            parts = []
            for row in range(2 * HELD):
                block = flat[pl.ds(sample * 4 + row, SLABS, stride=DEVICES // SLABS * 4), :]
                stacked = jnp.concatenate(lane_groups(block), 0).astype(BF16)
                parts.append(matmul(analysis_x[...], stacked))
            real = [parts[b][:MX] + parts[HELD + b][MX:] for b in range(HELD)]
            imag = [parts[HELD + b][:MX] - parts[b][MX:] for b in range(HELD)]
            turned = jnp.concatenate(real + imag, 0).T
            total = turned[:C] + turned[C:2 * C] + turned[2 * C:3 * C] + turned[3 * C:]
            target[sample] = total * scale

    def synthesise_x(turn):
        half = HELD * MX
        for sample in range(BATCHES):
            rounded = modes[sample].astype(BF16).astype(F32)
            turned = jnp.concatenate([rounded] * WIDTH, 0).T
            for part in range(2):
                for b in range(HELD):
                    real = turned[b * MX:(b + 1) * MX]
                    imag = turned[half + b * MX:half + (b + 1) * MX]
                    pair = [real, -imag] if part == 0 else [imag, real]
                    stacked = jnp.concatenate(
                        lane_groups(jnp.concatenate(pair, 0)), 0
                    ).astype(BF16)
                    flat[pl.ds(sample * 4 + part * HELD + b, SLABS, stride=DEVICES // SLABS * 4), :] = (
                        matmul(synthesis_x[...], stacked)
                    )

        def step(index, carry):
            slab = (me // BATCHES + index) % SLABS
            for sample in range(BATCHES):
                target = slab * BATCHES + sample
                sent[turn, target] = flat[
                    pl.ds(pl.multiple_of(target * 4, 4), 4), :
                ].astype(BF16)
                send(turn, target)
            return carry

        lax.fori_loop(0, SLABS, step, 0)

    def synthesise_z():
        def step(ky, carry):
            block = flat[pl.ds(pl.multiple_of(ky * 2 * MZ, 2 * MZ), 2 * MZ), :].T.astype(BF16)
            grid[ky] = matmul(block, synthesis_z[...])
            return carry

        lax.fori_loop(0, MY, step, 0)

    def synthesise_y(finish):
        def step(index, carry):
            pair = (index // GROUPS) * 2
            group = index % GROUPS
            columns = []
            for inner in range(2):
                row = pl.multiple_of((pair + inner) * C + group * GROUP, GROUP)
                halves = [
                    grid[:, pl.ds(row, GROUP), part * NZ:(part + 1) * NZ].reshape(MY * GROUP, NZ)
                    for part in range(2)
                ]
                columns.append(jnp.concatenate(halves, 0).astype(BF16))
            result[...] = matmul(synthesis_y[...], jnp.concatenate(columns, 1))

            def one(channel, carry):
                rows = pl.ds(pl.multiple_of(channel * NY, NY), NY)
                for inner in range(2):
                    finish(
                        group * GROUP + channel,
                        pair + inner,
                        result[rows, inner * NZ:(inner + 1) * NZ],
                    )
                return carry

            lax.fori_loop(0, GROUP, one, 0)
            return carry

        lax.fori_loop(0, 2 * GROUPS, step, 0)

    def pointwise(source, weight):
        spread_map[...] = spread(weight)

        def step(index, carry):
            pair = (index // (NY // BAND)) * 2
            band = pl.ds(pl.multiple_of((index % (NY // BAND)) * BAND, BAND), BAND)
            columns = [source[:, pair + inner, band, :].reshape(C * BAND, NZ) for inner in range(2)]
            product = matmul(spread_map[...], jnp.concatenate(columns, 1))
            for inner in range(2):
                linear[:, pair + inner, band, :] = product[
                    :, inner * NZ:(inner + 1) * NZ
                ].reshape(C, BAND, NZ)
            return carry

        lax.fori_loop(0, 2 * (NY // BAND), step, 0)

    def double_weights(channel, carry):
        for part in range(2):
            block = weights[part, channel].astype(F32)
            doubled[part, channel] = jnp.concatenate([block, block], 1)
        return carry

    lower = lax.broadcasted_iota(jnp.int32, (C, 2 * HELD * MX), 1) < HELD * MX

    def swapped(block):
        return pltpu.roll(block, HELD * MX, 1)

    def mix():
        for sample in range(BATCHES):
            turned = swapped(values[sample])
            grads[sample] = jnp.where(lower, -turned, turned)

        def step(channel, totals):
            real, imag = doubled[0, channel], doubled[1, channel]
            return tuple(
                totals[sample]
                + real * values[sample, pl.ds(channel, 1), :]
                + imag * grads[sample, pl.ds(channel, 1), :]
                for sample in range(BATCHES)
            )

        start = tuple(jnp.zeros((C, 2 * HELD * MX), F32) for _ in range(BATCHES))
        totals = lax.fori_loop(0, C, step, start)
        for sample in range(BATCHES):
            modes[sample] = totals[sample]

    def turned_grads(sample):
        turned = swapped(grads[sample])
        return jnp.where(lower, turned, -turned)

    def back_mix():
        for sample in range(BATCHES):
            straight, other = grads[sample], turned_grads(sample)

            def step(channel, carry):
                product = doubled[0, channel] * straight + doubled[1, channel] * other
                modes[sample, pl.ds(channel, 1), :] = jnp.sum(product, 0, keepdims=True)
                return carry

            lax.fori_loop(0, C, step, 0)

    def weight_products():
        for sample in range(BATCHES):
            turned = swapped(values[sample])
            modes[sample] = jnp.where(lower, values[sample], turned)
            values[sample] = jnp.where(lower, turned, values[sample])
        straight = [grads[sample] for sample in range(BATCHES)]
        other = [turned_grads(sample) for sample in range(BATCHES)]

        def step(channel, carry):
            total = jnp.zeros((C, 2 * HELD * MX), F32)
            for sample in range(BATCHES):
                total = total + straight[sample] * modes[sample, pl.ds(channel, 1), :]
                total = total + other[sample] * values[sample, pl.ds(channel, 1), :]
            weight_grad[0, channel] = total[:, :HELD * MX]
            weight_grad[1, channel] = total[:, HELD * MX:]
            return carry

        lax.fori_loop(0, C, step, 0)

    analyse_y(fields)
    pl.semaphore_wait(barrier, DEVICES - 1)
    analyse_z(0)
    pointwise(fields, forward_map[...])
    lax.fori_loop(0, C, double_weights, 0)
    receive(0)
    analyse_x(values, SCALE_IN)
    mix()
    synthesise_x(1)
    receive(1)
    synthesise_z()

    def forward_finish(channel, x, part):
        slopes = gelu_slope(linear[channel, x] + part * SCALE_OUT)
        slope[channel, x] = (cotangent[channel, x].astype(F32) * slopes).astype(BF16)

    synthesise_y(forward_finish)
    analyse_y(slope)
    analyse_z(2)
    pointwise(slope, backward_map[...])
    receive(2)
    analyse_x(grads, SCALE_OUT)
    back_mix()
    synthesise_x(3)
    weight_products()
    receive(3)
    synthesise_z()

    def backward_finish(channel, x, part):
        field_grad[channel, x] = (linear[channel, x] + part * SCALE_IN).astype(BF16)

    synthesise_y(backward_finish)
    some = pl.ds(0, DEVICES - 1)
    for turn in range(4):
        pltpu.make_async_copy(
            sent.at[turn, some], got.at[turn, some], send_sem.at[turn]
        ).wait()


def body(fields, cotangent, local_weight, spectral_weight):
    shape = (C, WIDTH, NY, NZ)
    lanes = 2 * HELD * MX
    operands = (
        fields.reshape(shape), cotangent.reshape(shape), local_weight.T, local_weight,
        spectral_weight, *make_tables(),
    )
    field_grad, weight_grad = pl.pallas_call(
        kernel,
        out_shape=(
            jax.ShapeDtypeStruct(shape, BF16),
            jax.ShapeDtypeStruct((2, C, C, HELD * MX), F32),
        ),
        in_specs=[pl.BlockSpec(memory_space=pltpu.VMEM)] * len(operands),
        out_specs=[pl.BlockSpec(memory_space=pltpu.VMEM)] * 2,
        scratch_shapes=[
            pltpu.VMEM((4, DEVICES, 4, 128), BF16),
            pltpu.VMEM((4, DEVICES, 4, 128), BF16),
            pltpu.VMEM((MY, WIDTH * C, 2 * NZ), F32),
            pltpu.VMEM((DEVICES * 4, 128), F32),
            pltpu.VMEM(shape, F32),
            pltpu.VMEM(shape, BF16),
            pltpu.VMEM((2, C, C, lanes), F32),
            pltpu.VMEM((BATCHES, C, lanes), F32),
            pltpu.VMEM((BATCHES, C, lanes), F32),
            pltpu.VMEM((BATCHES, C, lanes), F32),
            pltpu.VMEM((GROUP * NY, 2 * NZ), F32),
            pltpu.VMEM((C * BAND, C * BAND), BF16),
            pltpu.SemaphoreType.DMA((4,)),
            pltpu.SemaphoreType.DMA((4,)),
            pltpu.SemaphoreType.DMA((4,)),
        ],
        compiler_params=pltpu.CompilerParams(
            collective_id=0, has_side_effects=True, vmem_limit_bytes=60 << 20
        ),
    )(*operands)
    return (field_grad.reshape(fields.shape), weight_grad)


def solution(mesh):
    placed = (
        P("batch", None, "slab", None, None),
        P("batch", None, "slab", None, None),
        P(),
        P(None, None, None, ("slab", "batch")),
    )
    return jax.shard_map(
        body,
        mesh=mesh,
        in_specs=placed,
        out_specs=(P("batch", None, "slab", None, None), P(None, None, None, ("slab", "batch"))),
        check_vma=False,
    )
```

time: 637 us -> 121 us (0.19); the launches traced: 629 us -> 121 us
  waiting for transfers between devices: 424 us -> 0 us
  Pallas kernels: 0 us -> 113 us
  local copies, waits for them, and re-layouts: 102 us -> 7.22 us
  matrix products: 67.7 us -> 0 us
  other arithmetic: 18.6 us -> 0 us
  between operations: 15.9 us -> 0.65 us
    reduce_scatter x2 -> x0, waiting for transfers between devices: 277 us -> none  [analyse(): lax.psum_scatter(partial_sum, 'slab', scatter_dimension=3, tiled=True)]
    all_gather x3 -> x0, waiting for transfers between devices: 127 us -> none  [the longest x2 127 us: synthesise(): whole = lax.all_gather(modes_part, 'slab', axis=3, tiled=True)]
    pallas_call x0 -> x1, Pallas kernels: none -> 113 us  [body(): pl.pallas_call(kernel, out_shape=(jax.ShapeDtypeStruct(shape, BF16), jax....]
    dot_general x12 -> x0, matrix products: 67.7 us -> none  [contract(): return jnp.einsum(formula, left, right, preferred_element_type=jnp.float32)]
    reshape x2 -> x0, local copies, waits for them, and re-layouts: 26 us -> none  [analyse(): partial_sum = partial_sum.reshape(samples, channels, 2, MY * MZ * MX)]
    another operation x6 -> x0, local copies, waits for them, and re-layouts: 24.2 us -> none
    transpose x2 -> x0, local copies, waits for them, and re-layouts: 20.9 us -> none  [contract(): return jnp.einsum(formula, left, right, preferred_element_type=jnp.float32)]
    unnamed x7 -> x0, waiting for transfers between devices: 20.6 us -> none
  transfers between devices with their start and end apart: 6 -> 0, of which waited for: 5 -> 0; matrix products, arithmetic and copies ran while one was open for 2% -> 0% of each run, Pallas kernels for 0% -> 0%
where the time goes in v2:
time: 121 us
  Pallas kernels  113 us (93%)
  local copies, waits for them, and re-layouts  7.22 us (6%)
    pallas_call x1, Pallas kernels, body(): pl.pallas_call(kernel, out_shape=(jax.ShapeDtypeStruct(shape, BF16), jax....  113 us
    unnamed x5, local copies, waits for them, and re-layouts  7.22 us

profile of v2, /device:TPU:1, one launch (start us, length us, event | category | flops | bytes accessed | tf_op | source)
XLA Modules:
  0.0 121.0 jit_solution(15126772987985677426)
XLA Ops:
  0.6 1.4 %copy.12 = bf16[32,32]{0,1:T(8,128)(2,1)} copy(bf16[32,32]{1,0:T(8,128)(2,1)} %backward_map.1) | data formatting | bytes 4096 | tf_op args[2]
  2.0 113.1 %shard_map.113 = (bf16[32,4,128,128]{3,2,1,0:T(8,128)(2,1)}, f32[2,32,32,64]{3,2,1,0:T(8,128)}) custom-call(bf16[32,4,128,128]{3,2,1,0:T(8,128)(2,1)} %bitcast.4, bf16[32,4,128,128]{3,2,1,0:T(8,128)(2,1)} %bitcast.5, bf16[32,32]{1,0:T(8,128)(2,1)} %bitcast.7, bf16[32,32]{1,0:T(8,128)(2,1)} %backward_map.1, bf16[2,32,32,64]{3,2,1,0:T(8,128)(2,1)} %weights.1, ...), custom_call_target="tpu_custom_call" | custom-call | tf_op jit(solution)/shard_map/pallas_call | solution.py:398
  115.1 0.0 copy-start
  115.1 4.9 %copy.15 = bf16[1,32,4,128,128]{4,3,2,1,0:T(8,128)(2,1)} copy(bf16[1,32,4,128,128]{4,3,2,1,0:T(8,128)(2,1)} %bitcast.6) | data formatting | bytes 8388608
  120.0 0.0 copy-done
  120.0 1.0 copy.16
Async XLA Ops:
  115.1 4.9 %copy-start = (f32[2,32,32,64]{3,2,1,0:T(8,128)S(1)}, f32[2,32,32,64]{3,2,1,0:T(8,128)}, u32[]{:S(2)}) copy-start(f32[2,32,32,64]{3,2,1,0:T(8,128)} %get-tuple-element.9) | copy-start | bytes 1572868

commit v3 on v2

--- a/solution.py
+++ b/solution.py
@@ -26,6 +26,7 @@
 GROUP = 8
 GROUPS = C // GROUP
 BAND = 16
+SOME_KY = 4
 MESH = pl.DeviceIdType.MESH
 F32 = jnp.float32
 BF16 = jnp.bfloat16
@@ -54,6 +55,7 @@
     analysis_z = analysis_z.reshape(2, HIGH, HELD, 2 * NZ).transpose(1, 0, 2, 3).reshape(2 * MZ, 2 * NZ)
     synthesis_z = np.stack([np.stack([cos_z, sin_z], 1), np.stack([-sin_z, cos_z], 1)])
     synthesis_z = synthesis_z.reshape(2, HIGH, HELD, 2 * NZ).transpose(1, 0, 2, 3).reshape(2 * MZ, 2 * NZ)
+    synthesis_z = np.kron(np.eye(SOME_KY, dtype=np.float32), synthesis_z)
     both_x = np.stack([cos_x, sin_x]).reshape(2, MX, SLABS, WIDTH).transpose(0, 1, 3, 2)
     analysis_x = both_x.reshape(2 * MX, WIDTH * SLABS)
     synthesis_x = both_x.transpose(3, 2, 0, 1).reshape(SLABS, WIDTH * 2 * MX)
@@ -82,7 +84,7 @@
     return [jnp.where(lanes == group, value, 0.0) for group in range(WIDTH)]
 
 
-def spread(weight):
+def spread(weight, turned):
     rows = C * BAND
     left = (
         lax.broadcasted_iota(jnp.int32, (rows, C), 0) // BAND
@@ -92,7 +94,9 @@
         lax.broadcasted_iota(jnp.int32, (C, rows), 1) // BAND
         == lax.broadcasted_iota(jnp.int32, (C, rows), 0)
     ).astype(F32).astype(BF16)
-    whole = matmul(matmul(left, weight).astype(BF16), right)
+    side = 1 if turned else 0
+    tall = lax.dot_general(left, weight, (((1,), (side,)), ((), ())), preferred_element_type=F32)
+    whole = matmul(tall.astype(BF16), right)
     same = (
         lax.broadcasted_iota(jnp.int32, (rows, rows), 0) % BAND
         == lax.broadcasted_iota(jnp.int32, (rows, rows), 1) % BAND
@@ -100,18 +104,81 @@
     return jnp.where(same, whole, 0.0).astype(BF16)
 
 
+def unpack(source, flat):
+    def step(index, carry):
+        for inner in range(8):
+            tile = index * 8 + inner
+            flat[pl.ds(pl.multiple_of(tile * 4, 4), 4), :] = source[tile].astype(F32)
+        return carry
+
+    lax.fori_loop(0, DEVICES // 8, step, 0)
+
+
+def synthesise_z(flat, grid, table):
+    rows = SOME_KY * 2 * MZ
+
+    def step(index, carry):
+        block = flat[pl.ds(pl.multiple_of(index * rows, rows), rows), :].T.astype(BF16)
+        second = matmul(block, table[...])
+        for inner in range(SOME_KY):
+            grid[index * SOME_KY + inner] = second[:, inner * 2 * NZ:(inner + 1) * 2 * NZ]
+        return carry
+
+    lax.fori_loop(0, MY // SOME_KY, step, 0)
+
+
+def synthesise_y(grid, table, result, finish):
+    def step(index, carry):
+        pair = (index // GROUPS) * 2
+        group = index % GROUPS
+        columns = []
+        for inner in range(2):
+            row = pl.multiple_of((pair + inner) * C + group * GROUP, GROUP)
+            halves = [
+                grid[:, pl.ds(row, GROUP), part * NZ:(part + 1) * NZ].reshape(MY * GROUP, NZ)
+                for part in range(2)
+            ]
+            columns.append(jnp.concatenate(halves, 0).astype(BF16))
+        result[...] = matmul(table[...], jnp.concatenate(columns, 1))
+        finish(group * GROUP, pair, index)
+        return carry
+
+    lax.fori_loop(0, 2 * GROUPS, step, 0)
+
+
+def each_plane(result, apply):
+    def one(channel, carry):
+        rows = pl.ds(pl.multiple_of(channel * NY, NY), NY)
+        for inner in range(2):
+            apply(channel, inner, result[rows, inner * NZ:(inner + 1) * NZ])
+        return carry
+
+    lax.fori_loop(0, GROUP, one, 0)
+
+
 def kernel(
-    fields, cotangent, forward_map, backward_map, weights,
-    analysis_y, synthesis_y, analysis_z, synthesis_z, analysis_x, synthesis_x,
-    field_grad, weight_grad,
-    sent, got, grid, flat, linear, slope, doubled, values, grads, modes, result, spread_map,
-    send_sem, recv_sem, own_sem,
+    fields_hbm, cotangent_hbm, weights_hbm, analysis_y_hbm, synthesis_y_hbm, synthesis_z_hbm,
+    local_weight, analysis_z, analysis_x, synthesis_x,
+    through_hbm, last, weight_part,
+    fields, cotangent, weights, analysis_y, synthesis_y, synthesis_z,
+    sent, got, grid, flat, linear, slope, through, doubled, values, grads, modes, result,
+    spread_map, send_sem, recv_sem, own_sem, load_sem, store_sem,
 ):
     me = lax.axis_index("slab") * BATCHES + lax.axis_index("batch")
 
     def place(index):
         return (index // BATCHES, index % BATCHES)
 
+    loads = [
+        pltpu.make_async_copy(source, target, load_sem.at[index])
+        for index, (source, target) in enumerate((
+            (analysis_y_hbm, analysis_y), (fields_hbm, fields), (weights_hbm, weights),
+            (synthesis_z_hbm, synthesis_z), (synthesis_y_hbm, synthesis_y),
+            (cotangent_hbm, cotangent),
+        ))
+    ]
+    for load in loads:
+        load.start()
     barrier = pltpu.get_barrier_semaphore()
 
     def greet(step, carry):
@@ -140,20 +207,17 @@
                 sent.at[turn, me], got.at[turn, me], own_sem.at[turn]
             ).start()
 
-    def receive(turn):
+    def wait_messages(turn):
         pltpu.make_async_copy(sent.at[turn, me], got.at[turn, me], own_sem.at[turn]).wait()
         some = pl.ds(0, DEVICES - 1)
         pltpu.make_async_copy(
             sent.at[turn, some], got.at[turn, some], recv_sem.at[turn]
         ).wait()
 
-        def unpack(step, carry):
-            for inner in range(8):
-                index = step * 8 + inner
-                flat[pl.ds(pl.multiple_of(index * 4, 4), 4), :] = got[turn, index].astype(F32)
-            return carry
-
-        lax.fori_loop(0, DEVICES // 8, unpack, 0)
+
+    def receive(turn):
+        wait_messages(turn)
+        unpack(got.at[turn], flat)
 
     def analyse_y(source):
         def step(index, carry):
@@ -177,18 +241,27 @@
 
     def analyse_z(turn):
         def step(index, carry):
-            ky = (me // HIGH + index) % MY
-            first = grid[ky].astype(BF16)
-            second = lax.dot_general(
-                analysis_z[...], first, (((1,), (1,)), ((), ())), preferred_element_type=F32
-            )
-            for high in range(HIGH):
-                target = ky * HIGH + high
-                sent[turn, target] = second[4 * high:4 * high + 4].astype(BF16)
-                send(turn, target)
+            batch = [(me // HIGH + index * SOME_KY + inner) % MY for inner in range(SOME_KY)]
+            seconds = [
+                lax.dot_general(
+                    analysis_z[...], grid[ky].astype(BF16), (((1,), (1,)), ((), ())),
+                    preferred_element_type=F32,
+                )
+                for ky in batch
+            ]
+            for ky, second in zip(batch, seconds):
+                for high in range(HIGH):
+                    sent[turn, ky * HIGH + high] = second[4 * high:4 * high + 4].astype(BF16)
+
+            def start(high, carry):
+                for ky in batch:
+                    send(turn, ky * HIGH + high)
+                return carry
+
+            lax.fori_loop(0, HIGH, start, 0)
             return carry
 
-        lax.fori_loop(0, MY, step, 0)
+        lax.fori_loop(0, MY // SOME_KY, step, 0)
 
     def analyse_x(target, scale):
         for sample in range(BATCHES):
@@ -232,45 +305,8 @@
 
         lax.fori_loop(0, SLABS, step, 0)
 
-    def synthesise_z():
-        def step(ky, carry):
-            block = flat[pl.ds(pl.multiple_of(ky * 2 * MZ, 2 * MZ), 2 * MZ), :].T.astype(BF16)
-            grid[ky] = matmul(block, synthesis_z[...])
-            return carry
-
-        lax.fori_loop(0, MY, step, 0)
-
-    def synthesise_y(finish):
-        def step(index, carry):
-            pair = (index // GROUPS) * 2
-            group = index % GROUPS
-            columns = []
-            for inner in range(2):
-                row = pl.multiple_of((pair + inner) * C + group * GROUP, GROUP)
-                halves = [
-                    grid[:, pl.ds(row, GROUP), part * NZ:(part + 1) * NZ].reshape(MY * GROUP, NZ)
-                    for part in range(2)
-                ]
-                columns.append(jnp.concatenate(halves, 0).astype(BF16))
-            result[...] = matmul(synthesis_y[...], jnp.concatenate(columns, 1))
-
-            def one(channel, carry):
-                rows = pl.ds(pl.multiple_of(channel * NY, NY), NY)
-                for inner in range(2):
-                    finish(
-                        group * GROUP + channel,
-                        pair + inner,
-                        result[rows, inner * NZ:(inner + 1) * NZ],
-                    )
-                return carry
-
-            lax.fori_loop(0, GROUP, one, 0)
-            return carry
-
-        lax.fori_loop(0, 2 * GROUPS, step, 0)
-
-    def pointwise(source, weight):
-        spread_map[...] = spread(weight)
+    def pointwise(source, turned, target):
+        spread_map[...] = spread(local_weight[...], turned)
 
         def step(index, carry):
             pair = (index // (NY // BAND)) * 2
@@ -278,9 +314,9 @@
             columns = [source[:, pair + inner, band, :].reshape(C * BAND, NZ) for inner in range(2)]
             product = matmul(spread_map[...], jnp.concatenate(columns, 1))
             for inner in range(2):
-                linear[:, pair + inner, band, :] = product[
+                target[:, pair + inner, band, :] = product[
                     :, inner * NZ:(inner + 1) * NZ
-                ].reshape(C, BAND, NZ)
+                ].reshape(C, BAND, NZ).astype(target.dtype)
             return carry
 
         lax.fori_loop(0, 2 * (NY // BAND), step, 0)
@@ -343,44 +379,48 @@
             for sample in range(BATCHES):
                 total = total + straight[sample] * modes[sample, pl.ds(channel, 1), :]
                 total = total + other[sample] * values[sample, pl.ds(channel, 1), :]
-            weight_grad[0, channel] = total[:, :HELD * MX]
-            weight_grad[1, channel] = total[:, HELD * MX:]
+            weight_part[channel] = total
             return carry
 
         lax.fori_loop(0, C, step, 0)
 
+    def forward_finish(channel, x, index):
+        def apply(offset, inner, part):
+            place = (channel + offset, x + inner)
+            slopes = gelu_slope(linear[place] + part * SCALE_OUT)
+            slope[place] = (cotangent[place].astype(F32) * slopes).astype(BF16)
+
+        each_plane(result, apply)
+
+    loads[0].wait()
+    loads[1].wait()
     analyse_y(fields)
     pl.semaphore_wait(barrier, DEVICES - 1)
     analyse_z(0)
-    pointwise(fields, forward_map[...])
+    pointwise(fields, True, linear)
+    for load in loads[2:]:
+        load.wait()
     lax.fori_loop(0, C, double_weights, 0)
     receive(0)
     analyse_x(values, SCALE_IN)
     mix()
     synthesise_x(1)
     receive(1)
-    synthesise_z()
-
-    def forward_finish(channel, x, part):
-        slopes = gelu_slope(linear[channel, x] + part * SCALE_OUT)
-        slope[channel, x] = (cotangent[channel, x].astype(F32) * slopes).astype(BF16)
-
-    synthesise_y(forward_finish)
+    synthesise_z(flat, grid, synthesis_z)
+    synthesise_y(grid, synthesis_y, result, forward_finish)
     analyse_y(slope)
     analyse_z(2)
-    pointwise(slope, backward_map[...])
+    pointwise(slope, False, through)
+    store = pltpu.make_async_copy(through, through_hbm, store_sem)
+    store.start()
     receive(2)
     analyse_x(grads, SCALE_OUT)
     back_mix()
     synthesise_x(3)
     weight_products()
-    receive(3)
-    synthesise_z()
-
-    def backward_finish(channel, x, part):
-        field_grad[channel, x] = (linear[channel, x] + part * SCALE_IN).astype(BF16)
-
-    synthesise_y(backward_finish)
+    store.wait()
+    wait_messages(3)
+    last[...] = got[3]
     some = pl.ds(0, DEVICES - 1)
     for turn in range(4):
         pltpu.make_async_copy(
@@ -388,27 +428,69 @@
         ).wait()
 
 
+def last_kernel(
+    messages, synthesis_z, synthesis_y, through_hbm, field_grad_hbm,
+    grid, flat, result, through, field_grad, load_sem, store_sem,
+):
+
+    def some(index):
+        return (pl.ds((index % GROUPS) * GROUP, GROUP), pl.ds((index // GROUPS) * 2, 2))
+
+    def load(index):
+        return pltpu.make_async_copy(
+            through_hbm.at[some(index)], through.at[some(index)], load_sem.at[index]
+        )
+
+    def store(index):
+        return pltpu.make_async_copy(
+            field_grad.at[some(index)], field_grad_hbm.at[some(index)], store_sem.at[index]
+        )
+
+    for index in range(2 * GROUPS):
+        load(index).start()
+    unpack(messages, flat)
+    synthesise_z(flat, grid, synthesis_z)
+
+    def finish(channel, x, index):
+        load(index).wait()
+
+        def apply(offset, inner, part):
+            place = (channel + offset, x + inner)
+            field_grad[place] = (through[place].astype(F32) + part * SCALE_IN).astype(BF16)
+
+        each_plane(result, apply)
+        store(index).start()
+
+    synthesise_y(grid, synthesis_y, result, finish)
+    for index in range(2 * GROUPS):
+        store(index).wait()
+
+
 def body(fields, cotangent, local_weight, spectral_weight):
     shape = (C, WIDTH, NY, NZ)
     lanes = 2 * HELD * MX
-    operands = (
-        fields.reshape(shape), cotangent.reshape(shape), local_weight.T, local_weight,
-        spectral_weight, *make_tables(),
+    analysis_y, synthesis_y, analysis_z, synthesis_z, analysis_x, synthesis_x = make_tables()
+    far = (
+        fields.reshape(shape), cotangent.reshape(shape), spectral_weight,
+        analysis_y, synthesis_y, synthesis_z,
     )
-    field_grad, weight_grad = pl.pallas_call(
+    near = (local_weight, analysis_z, analysis_x, synthesis_x)
+    in_vmem, anywhere = pl.BlockSpec(memory_space=pltpu.VMEM), pl.BlockSpec(memory_space=pl.ANY)
+    field_shape = jax.ShapeDtypeStruct(shape, BF16)
+    message_shape = jax.ShapeDtypeStruct((DEVICES, 4, 128), BF16)
+    part_shape = jax.ShapeDtypeStruct((C, C, lanes), F32)
+    through, messages, part = pl.pallas_call(
         kernel,
-        out_shape=(
-            jax.ShapeDtypeStruct(shape, BF16),
-            jax.ShapeDtypeStruct((2, C, C, HELD * MX), F32),
-        ),
-        in_specs=[pl.BlockSpec(memory_space=pltpu.VMEM)] * len(operands),
-        out_specs=[pl.BlockSpec(memory_space=pltpu.VMEM)] * 2,
-        scratch_shapes=[
+        out_shape=(field_shape, message_shape, part_shape),
+        in_specs=[anywhere] * len(far) + [in_vmem] * len(near),
+        out_specs=[anywhere, in_vmem, in_vmem],
+        scratch_shapes=[pltpu.VMEM(array.shape, BF16) for array in far] + [
             pltpu.VMEM((4, DEVICES, 4, 128), BF16),
             pltpu.VMEM((4, DEVICES, 4, 128), BF16),
             pltpu.VMEM((MY, WIDTH * C, 2 * NZ), F32),
             pltpu.VMEM((DEVICES * 4, 128), F32),
             pltpu.VMEM(shape, F32),
+            pltpu.VMEM(shape, BF16),
             pltpu.VMEM(shape, BF16),
             pltpu.VMEM((2, C, C, lanes), F32),
             pltpu.VMEM((BATCHES, C, lanes), F32),
@@ -419,11 +501,30 @@
             pltpu.SemaphoreType.DMA((4,)),
             pltpu.SemaphoreType.DMA((4,)),
             pltpu.SemaphoreType.DMA((4,)),
+            pltpu.SemaphoreType.DMA((len(far),)),
+            pltpu.SemaphoreType.DMA,
         ],
         compiler_params=pltpu.CompilerParams(
             collective_id=0, has_side_effects=True, vmem_limit_bytes=60 << 20
         ),
-    )(*operands)
+    )(*far, *near)
+    field_grad = pl.pallas_call(
+        last_kernel,
+        out_shape=field_shape,
+        in_specs=[in_vmem] * 3 + [anywhere],
+        out_specs=anywhere,
+        scratch_shapes=[
+            pltpu.VMEM((MY, WIDTH * C, 2 * NZ), F32),
+            pltpu.VMEM((DEVICES * 4, 128), F32),
+            pltpu.VMEM((GROUP * NY, 2 * NZ), F32),
+            pltpu.VMEM(shape, BF16),
+            pltpu.VMEM(shape, BF16),
+            pltpu.SemaphoreType.DMA((2 * GROUPS,)),
+            pltpu.SemaphoreType.DMA((2 * GROUPS,)),
+        ],
+        compiler_params=pltpu.CompilerParams(vmem_limit_bytes=60 << 20),
+    )(messages, synthesis_z, synthesis_y, through)
+    weight_grad = jnp.stack([part[:, :, :HELD * MX], part[:, :, HELD * MX:]], 0)
     return (field_grad.reshape(fields.shape), weight_grad)
 
 

time: 121 us -> 102 us (0.84)
  Pallas kernels: 113 us -> 99.5 us
  local copies, waits for them, and re-layouts: 7.22 us -> 0.21 us
    pallas_call x1 -> x2, Pallas kernels: 113 us -> 99.5 us  [the longest x1 89.9 us: body(): pl.pallas_call(kernel, out_shape=(field_shape, message_shape, part_shape)...]
    unnamed x5 -> x2, local copies, waits for them, and re-layouts: 7.22 us -> 0.01 us
where the time goes in v3:
time: 102 us; the launch traced here: 101 us
  Pallas kernels  99.5 us (98%)
  other arithmetic  1.08 us (1%)
    pallas_call x1, Pallas kernels, body(): pl.pallas_call(kernel, out_shape=(field_shape, message_shape, part_shape)...  89.9 us
    pallas_call x1, Pallas kernels, body(): pl.pallas_call(last_kernel, out_shape=field_shape, in_specs=[in_vmem] * 3...  9.64 us

profile of v3, /device:TPU:1, one launch (start us, length us, event | category | flops | bytes accessed | tf_op | source)
XLA Modules:
  0.0 101.5 jit_solution(245997783156160266)
XLA Ops:
  0.6 89.9 %shard_map.113 = (bf16[32,4,128,128]{3,2,1,0:T(8,128)(2,1)}, bf16[256,4,128]{2,1,0:T(4,128)(2,1)}, f32[32,32,128]{2,1,0:T(8,128)}) custom-call(bf16[32,4,128,128]{3,2,1,0:T(8,128)(2,1)} %bitcast.7, bf16[32,4,128,128]{3,2,1,0:T(8,128)(2,1)} %bitcast.8, bf16[2,32,32,64]{3,2,1,0:T(8,128)(2,1)} %weights_hbm.1, bf16[512,1024]{1,0:T(8,128)(2,1)} %constant.12.clone.analysis_y_hbm, ...), custom_call_target="tpu_custom_call" | custom-call | tf_op jit(solution)/shard_map/pallas_call | solution.py:482
  90.5 0.0 copy-start
  90.5 9.6 %shard_map.114 = bf16[32,4,128,128]{3,2,1,0:T(8,128)(2,1)} custom-call(bf16[256,4,128]{2,1,0:T(4,128)(2,1)} %get-tuple-element.5.messages, bf16[128,1024]{1,0:T(8,128)(2,1)} %constant.14.clone.synthesis_z_hbm.synthesis_z, bf16[1024,512]{1,0:T(8,128)(2,1)} %constant.13.clone.synthesis_y_hbm.synthesis_y, bf16[32,4,128,128]{3,2,1,0:T(8,128)(2,1)} %get-tuple-element.6.through_hbm), custom_call_target="tpu_custom_call" | custom-call | tf_op jit(solution)/shard_map/pallas_call | solution.py:511
  100.2 0.0 copy-done
  100.2 0.2 slice_bitcast_fusion.1
  100.4 1.1 %pad_maximum_fusion = f32[2,32,32,64]{3,2,1,0:T(8,128)} fusion(f32[1,32,32,64]{3,2,1,0:T(8,128)S(1)} %get-tuple-element.9, f32[1,32,32,64]{3,2,1,0:T(8,128)S(1)} %get-tuple-element.8), kind=kLoop, calls=%fused_computation | loop fusion | flops 131072 | bytes 1048576 | tf_op jit(solution)/shard_map/stack | solution.py:527
Async XLA Ops:
  90.5 9.7 %copy-start = (f32[32,32,128]{2,1,0:T(8,128)S(1)}, f32[32,32,128]{2,1,0:T(8,128)}, u32[]{:S(2)}) copy-start(f32[32,32,128]{2,1,0:T(8,128)} %get-tuple-element.7) | copy-start | bytes 1572868

commit v4 on v3

v4 whole, which is shorter than its diff:
```python
import math

import jax
import jax.numpy as jnp
import ml_dtypes
import numpy as np
from jax import lax
from jax.experimental import pallas as pl
from jax.experimental.pallas import tpu as pltpu
from jax.sharding import PartitionSpec as P

C = 32
NX = 256
NY = 128
NZ = 128
MX = 32
MY = 32
MZ = 16
SLABS = 64
BATCHES = 4
WIDTH = NX // SLABS
HELD = 2
HIGH = MZ // HELD
MODES = HELD * MX
LANES = 2 * MODES
ROWS = 2 * BATCHES
GROUP = 8
GROUPS = C // GROUP
BAND = 16
SOME_KY = 8
MESH = pl.DeviceIdType.MESH
F32 = jnp.float32
BF16 = jnp.bfloat16
SCALE_IN = 1.0 / math.sqrt(NX * NY * NZ)
SCALE_OUT = 1.0 / math.sqrt(MX * MY * MZ * C)


def wave_table(number, length, signed):
    numbers = np.arange(number)
    if signed:
        numbers = np.where(numbers < number // 2, numbers, numbers - number)
    phases = np.mod(numbers[:, None] * np.arange(length)[None, :], length).astype(np.float32)
    angles = phases * np.float32(2.0 * math.pi / length)
    return (np.cos(angles).astype(np.float32), np.sin(angles).astype(np.float32))


def make_tables():
    cos_y, sin_y = wave_table(MY, NY, True)
    cos_z, sin_z = wave_table(MZ, NZ, False)
    cos_x, sin_x = wave_table(MX, NX, True)
    eye = np.eye(GROUP, dtype=np.float32)
    pair_y = np.stack([cos_y, -sin_y])
    analysis_y = np.einsum("pky,ab->pkaby", pair_y, eye).reshape(2 * MY * GROUP, GROUP * NY)
    synthesis_y = np.einsum("pky,ab->aypkb", pair_y, eye).reshape(GROUP * NY, 2 * MY * GROUP)
    both_z = np.stack([np.stack([cos_z, sin_z], 1), np.stack([-sin_z, cos_z], 1)])
    both_z = both_z.reshape(2, HIGH, HELD, 2 * NZ)
    analysis_z = both_z.transpose(2, 1, 0, 3).reshape(2 * MZ, 2 * NZ)
    several = np.eye(SOME_KY, dtype=np.float32)
    synthesis_z = np.einsum("qhlw,ab->lahqbw", both_z, several)
    synthesis_z = synthesis_z.reshape(SOME_KY * 2 * MZ, SOME_KY * 2 * NZ)
    both_x = np.stack([cos_x, sin_x]).reshape(2, MX, SLABS, WIDTH).transpose(0, 1, 3, 2)
    analysis_x = both_x.reshape(2 * MX, WIDTH * SLABS)
    synthesis_x = both_x.reshape(2, MX, 2, 2, SLABS).transpose(2, 4, 3, 0, 1)
    synthesis_x = synthesis_x.reshape(2 * SLABS, 2 * 2 * MX)
    tables = (analysis_y, synthesis_y, analysis_z, synthesis_z, analysis_x, synthesis_x)
    return tuple(np.ascontiguousarray(table).astype(ml_dtypes.bfloat16) for table in tables)


def matmul(left, right):
    return jnp.dot(left, right, preferred_element_type=F32)


def gelu_slope(values):
    size = jnp.abs(values)
    below = 1.0 + (0.3275911 / math.sqrt(2.0)) * size
    inverse = pl.reciprocal(below, approx=True)
    inverse = inverse * (2.0 - below * inverse)
    tail = 0.5 * 1.061405429 * inverse - 0.5 * 1.453152027
    tail = tail * inverse + 0.5 * 1.421413741
    tail = tail * inverse - 0.5 * 0.284496736
    tail = tail * inverse + 0.5 * 0.254829592
    tail = tail * inverse - size * (1.0 / math.sqrt(2.0 * math.pi))
    below = jnp.exp2((-0.5 / math.log(2.0)) * (values * values)) * tail
    return jnp.where(values >= 0.0, 1.0 - below, below)


def lane_index(shape):
    return lax.broadcasted_iota(jnp.int32, shape, len(shape) - 1)


def split_cells(value):
    second = (lane_index(value.shape) // C) % 2 == 1
    return [jnp.where(second, 0.0, value), jnp.where(second, value, 0.0)]


def spread(weight, turned):
    rows = C * BAND
    left = (
        lax.broadcasted_iota(jnp.int32, (rows, C), 0) // BAND
        == lax.broadcasted_iota(jnp.int32, (rows, C), 1)
    ).astype(F32).astype(BF16)
    right = (
        lax.broadcasted_iota(jnp.int32, (C, rows), 1) // BAND
        == lax.broadcasted_iota(jnp.int32, (C, rows), 0)
    ).astype(F32).astype(BF16)
    side = 1 if turned else 0
    tall = lax.dot_general(left, weight, (((1,), (side,)), ((), ())), preferred_element_type=F32)
    whole = matmul(tall.astype(BF16), right)
    same = (
        lax.broadcasted_iota(jnp.int32, (rows, rows), 0) % BAND
        == lax.broadcasted_iota(jnp.int32, (rows, rows), 1) % BAND
    )
    return jnp.where(same, whole, 0.0).astype(BF16)


def unpack(source, flat):
    def step(index, carry):
        for inner in range(8):
            tile = index * 8 + inner
            flat[pl.ds(pl.multiple_of(tile * ROWS, ROWS), ROWS), :] = source[tile].astype(F32)
        return carry

    lax.fori_loop(0, SLABS // 8, step, 0)


def synthesise_z(flat, grid, table):
    rows = SOME_KY * MZ
    half = LANES // 2
    batches = MY // SOME_KY
    blocks = []
    for batch in range(batches):
        turned = flat[pl.ds(batch * rows, rows), :].T
        blocks.append(jnp.concatenate([turned[:half], turned[half:]], 1))
    left = jnp.concatenate(blocks, 0).astype(BF16)
    for inner in range(SOME_KY):
        second = matmul(left, table[:, inner * 2 * NZ:(inner + 1) * 2 * NZ])
        for batch in range(batches):
            grid[batch * SOME_KY + inner] = second[batch * half:(batch + 1) * half]


def synthesise_y(grid, table, result, finish):
    def step(group, carry):
        columns = []
        for inner in range(2):
            row = pl.multiple_of(inner * C + group * GROUP, GROUP)
            halves = [
                grid[:, pl.ds(row, GROUP), part * NZ:(part + 1) * NZ].reshape(MY * GROUP, NZ)
                for part in range(2)
            ]
            columns.append(jnp.concatenate(halves, 0).astype(BF16))
        result[...] = matmul(table[...], jnp.concatenate(columns, 1))
        finish(group)
        return carry

    lax.fori_loop(0, GROUPS, step, 0)


def each_plane(result, apply):
    def one(channel, carry):
        rows = pl.ds(pl.multiple_of(channel * NY, NY), NY)
        for inner in range(2):
            apply(channel, inner, result[rows, inner * NZ:(inner + 1) * NZ])
        return carry

    lax.fori_loop(0, GROUP, one, 0)


def kernel(
    fields_hbm, cotangent_hbm, weights_hbm, analysis_y_hbm, synthesis_y_hbm, synthesis_z_hbm,
    local_weight, analysis_z, analysis_x, synthesis_x,
    through_hbm, last, weight_part_hbm,
    fields, cotangent, weights, analysis_y, synthesis_y, synthesis_z,
    sent, got, grid, flat, linear, slope, through, packed, doubled, values, grads, modes, result,
    spread_map, spectra, both, weight_part,
    send_sem, recv_sem, own_sem, load_sem, store_sem, pack_sem, part_sem,
):
    me = lax.axis_index("slab")
    sample = lax.axis_index("batch")
    cells = [(slice(None), pl.ds(2 * pair, 2)) for pair in range(2)]
    loads = [
        pltpu.make_async_copy(source, target, load_sem.at[index])
        for index, (source, target) in enumerate((
            (analysis_y_hbm, analysis_y), (fields_hbm.at[cells[0]], fields.at[cells[0]]),
            (weights_hbm, weights), (fields_hbm.at[cells[1]], fields.at[cells[1]]),
            (synthesis_z_hbm, synthesis_z), (synthesis_y_hbm, synthesis_y),
            (cotangent_hbm, cotangent),
        ))
    ]
    for load in loads[:3]:
        load.start()
    barrier = pltpu.get_barrier_semaphore()

    def greet(step, carry):
        pl.semaphore_signal(
            barrier, inc=1, device_id=((me + step) % SLABS, sample), device_id_type=MESH
        )
        return carry

    lax.fori_loop(1, SLABS, greet, 0)
    for step in range(1, BATCHES):
        pl.semaphore_signal(
            barrier, inc=1, device_id=(me, (sample + step) % BATCHES), device_id_type=MESH
        )

    def send(turn, pair, target):
        pltpu.make_async_remote_copy(
            src_ref=sent.at[turn, pair, target],
            dst_ref=got.at[turn, pair, me],
            send_sem=send_sem.at[turn, pair],
            recv_sem=recv_sem.at[turn, pair],
            device_id=(target, sample),
            device_id_type=MESH,
        ).start()

    def keep(turn, pair):
        pltpu.make_async_copy(
            sent.at[turn, pair, me], got.at[turn, pair, me], own_sem.at[turn, pair]
        ).start()

    some = pl.ds(0, SLABS - 1)

    def wait_messages(turn, pair):
        pltpu.make_async_copy(
            sent.at[turn, pair, me], got.at[turn, pair, me], own_sem.at[turn, pair]
        ).wait()
        pltpu.make_async_copy(
            sent.at[turn, pair, some], got.at[turn, pair, some], recv_sem.at[turn, pair]
        ).wait()

    def receive(turn, pair):
        wait_messages(turn, pair)
        unpack(got.at[turn, pair], flat.at[pair])

    def analyse_y(source, pair):
        def step(group, carry):
            channels = pl.ds(group * GROUP, GROUP)
            planes = [
                source[channels, 2 * pair + inner].reshape(GROUP * NY, NZ) for inner in range(2)
            ]
            first = matmul(analysis_y[...], jnp.concatenate(planes, 1))
            first = first.reshape(2, MY, GROUP, 2 * NZ)
            for inner in range(2):
                row = pl.multiple_of(inner * C + group * GROUP, GROUP)
                for part in range(2):
                    grid[:, pl.ds(row, GROUP), part * NZ:(part + 1) * NZ] = first[
                        part, :, :, inner * NZ:(inner + 1) * NZ
                    ]
            return carry

        lax.fori_loop(0, GROUPS, step, 0)

    def analyse_z(turn, pair):
        left = lane_index((MZ, LANES)) < LANES // 2

        def transform(index):
            batch = [(me // 2 + index * 4 + inner) % MY for inner in range(4)]
            for two in (batch[:2], batch[2:]):
                first = jnp.concatenate([grid[ky] for ky in two], 0).astype(BF16)
                second = lax.dot_general(
                    analysis_z[...], first, (((1,), (1,)), ((), ())), preferred_element_type=F32
                )
                upper, lower = second[:MZ], second[MZ:]
                ready = (
                    jnp.where(left, upper, pltpu.roll(lower, LANES // 2, 1)),
                    jnp.where(left, pltpu.roll(upper, LANES // 2, 1), lower),
                )
                for ky, message in zip(two, ready):
                    for side in range(2):
                        sent[turn, pair, 2 * ky + side] = message[
                            ROWS * side:ROWS * (side + 1)
                        ].astype(BF16)
            return batch

        def step(index, carry):
            for ky in transform(index):
                for side in range(2):
                    send(turn, pair, 2 * ky + side)
            return carry

        for ky in transform(0)[1:]:
            for side in range(2):
                send(turn, pair, 2 * ky + side)
        send(turn, pair, me + 1 - 2 * (me % 2))
        keep(turn, pair)
        lax.fori_loop(1, MY // 4, step, 0)

    def analyse_x(target, scale):
        for block in range(BATCHES):
            parts = []
            for part in range(2):
                cells = []
                for pair in range(2):
                    rows = pl.ds(block * 2 + part, SLABS, stride=ROWS)
                    cells += split_cells(flat[pair, rows, :])
                parts.append(matmul(analysis_x[...], jnp.concatenate(cells, 0).astype(BF16)))
            real = parts[0][:MX] + parts[1][MX:]
            imag = parts[1][:MX] - parts[0][MX:]
            turned = jnp.concatenate([real, imag], 0).T
            held = [
                turned[2 * C * b:2 * C * b + C] + turned[2 * C * b + C:2 * C * (b + 1)]
                for b in range(HELD)
            ]
            pieces = [held[b][:, part * MX:(part + 1) * MX] for part in range(2) for b in range(HELD)]
            target[block] = jnp.concatenate(pieces, 1) * scale

    def synthesise_x(turn):
        for block in range(BATCHES):
            rounded = modes[block].astype(BF16).astype(F32)
            tall = []
            for b in range(HELD):
                piece = jnp.concatenate([
                    rounded[:, part * MODES + b * MX:part * MODES + (b + 1) * MX]
                    for part in range(2)
                ], 1)
                tall += [piece, piece]
            turned = jnp.concatenate(tall, 0).T
            real, imag = turned[:MX], turned[MX:]
            for part in range(2):
                pair = [real, -imag] if part == 0 else [imag, real]
                stacked = jnp.concatenate(split_cells(jnp.concatenate(pair, 0)), 0).astype(BF16)
                product = matmul(synthesis_x[...], stacked)
                for half in range(2):
                    rows = pl.ds(block * 2 + part, SLABS, stride=ROWS)
                    flat[half, rows, :] = product[half * SLABS:(half + 1) * SLABS]

        for half in range(2):
            def pack(index, carry, half=half):
                for inner in range(8):
                    target = index * 8 + inner
                    sent[turn, half, target] = flat[
                        half, pl.ds(pl.multiple_of(target * ROWS, ROWS), ROWS), :
                    ].astype(BF16)
                return carry

            def step(index, carry, half=half):
                for inner in range(1, 10):
                    send(turn, half, (me + index * 9 + inner) % SLABS)
                return carry

            lax.fori_loop(0, SLABS // 8, pack, 0)
            lax.fori_loop(0, SLABS // 9, step, 0)
            keep(turn, half)

    def pointwise(source, turned, target):
        spread_map[...] = spread(local_weight[...], turned)

        def step(index, carry):
            pair = (index // (NY // BAND)) * 2
            band = pl.ds(pl.multiple_of((index % (NY // BAND)) * BAND, BAND), BAND)
            columns = [source[:, pair + inner, band, :].reshape(C * BAND, NZ) for inner in range(2)]
            product = matmul(spread_map[...], jnp.concatenate(columns, 1))
            for inner in range(2):
                target[:, pair + inner, band, :] = product[
                    :, inner * NZ:(inner + 1) * NZ
                ].reshape(C, BAND, NZ).astype(target.dtype)
            return carry

        lax.fori_loop(0, 2 * (NY // BAND), step, 0)

    def weight_copy(step):
        return pltpu.make_async_remote_copy(
            src_ref=packed.at[sample],
            dst_ref=packed.at[sample],
            send_sem=pack_sem.at[0],
            recv_sem=pack_sem.at[1],
            device_id=(me, (sample + step) % BATCHES),
            device_id_type=MESH,
        )

    def pack_weights(index, carry):
        for inner in range(8):
            channel = index * 8 + inner
            pieces = [weights[part, channel].astype(F32) for part in range(2)]
            packed[sample, channel] = jnp.concatenate(pieces, 1).astype(BF16)
        return carry

    three = pl.ds(0, BATCHES - 1)
    lower = lane_index((C, LANES)) < MODES

    def swapped(block):
        return pltpu.roll(block, MODES, 1)

    def double_weights(channel, carry):
        for block in range(BATCHES):
            both = packed[block, channel].astype(F32)
            turned = swapped(both)
            doubled[block, 0, channel] = jnp.where(lower, both, turned)
            doubled[block, 1, channel] = jnp.where(lower, turned, both)
        return carry

    def mix():
        for block in range(BATCHES):
            turned = swapped(values[block])
            both[0, block] = jnp.where(lower, -turned, turned)

        def step(channel, totals):
            row = pl.ds(channel, 1)
            return tuple(
                totals[block]
                + doubled[block, 0, channel] * values[block, row, :]
                + doubled[block, 1, channel] * both[0, block, row, :]
                for block in range(BATCHES)
            )

        start = tuple(jnp.zeros((C, LANES), F32) for _ in range(BATCHES))
        totals = lax.fori_loop(0, C, step, start)
        for block in range(BATCHES):
            modes[block] = totals[block]

    def turned_grads(block):
        turned = swapped(grads[block])
        return jnp.where(lower, turned, -turned)

    def back_mix():
        for block in range(BATCHES):
            straight, other = grads[block], turned_grads(block)

            def step(channel, carry, block=block, straight=straight, other=other):
                product = (
                    doubled[block, 0, channel] * straight + doubled[block, 1, channel] * other
                )
                modes[block, pl.ds(channel, 1), :] = jnp.sum(product, 0, keepdims=True)
                return carry

            lax.fori_loop(0, C, step, 0)

    def spectrum_copy(kind, source, step):
        return pltpu.make_async_remote_copy(
            src_ref=source.at[(sample + step) % BATCHES],
            dst_ref=spectra.at[kind, sample],
            send_sem=part_sem.at[kind, 0],
            recv_sem=part_sem.at[kind, 1],
            device_id=(me, (sample + step) % BATCHES),
            device_id_type=MESH,
        )

    def share(kind, source):
        for step in range(1, BATCHES):
            spectrum_copy(kind, source, step).start()
        spectra[kind, sample] = source[sample]

    def weight_products():
        for kind in range(2):
            pltpu.make_async_copy(
                values.at[three], spectra.at[kind, three], part_sem.at[kind, 1]
            ).wait()
        straight, other = [], []
        for part in range(BATCHES):
            turned = swapped(spectra[0, part])
            both[0, part] = jnp.where(lower, spectra[0, part], turned)
            both[1, part] = jnp.where(lower, turned, spectra[0, part])
            turned = swapped(spectra[1, part])
            straight.append(spectra[1, part])
            other.append(jnp.where(lower, turned, -turned))

        def step(channel, carry):
            row = pl.ds(channel, 1)
            total = jnp.zeros((C, LANES), F32)
            for part in range(BATCHES):
                total = total + straight[part] * both[0, part, row, :]
                total = total + other[part] * both[1, part, row, :]
            weight_part[channel] = total
            return carry

        lax.fori_loop(0, C, step, 0)

    def forward_half(pair, carry):
        receive(1, pair)
        synthesise_z(flat.at[pair], grid, synthesis_z)

        def finish(group):
            def apply(offset, inner, part):
                place = (group * GROUP + offset, 2 * pair + inner)
                slopes = gelu_slope(linear[place] + part * SCALE_OUT)
                slope[place] = (cotangent[place].astype(F32) * slopes).astype(BF16)

            each_plane(result, apply)

        synthesise_y(grid, synthesis_y, result, finish)
        analyse_y(slope, pair)
        analyse_z(2, pair)
        return carry

    loads[0].wait()
    loads[1].wait()
    for load in loads[3:]:
        load.start()
    analyse_y(fields, 0)
    loads[2].wait()
    lax.fori_loop(0, C // 8, pack_weights, 0)
    pl.semaphore_wait(barrier, SLABS - 1 + BATCHES - 1)
    for step in range(1, BATCHES):
        weight_copy(step).start()
    analyse_z(0, 0)
    loads[3].wait()
    analyse_y(fields, 1)
    analyse_z(0, 1)
    pointwise(fields, True, linear)
    for load in loads[4:]:
        load.wait()
    pltpu.make_async_copy(packed.at[three], packed.at[three], pack_sem.at[1]).wait()
    lax.fori_loop(0, C, double_weights, 0)
    receive(0, 0)
    receive(0, 1)
    analyse_x(values, SCALE_IN)
    share(0, values)
    mix()
    synthesise_x(1)
    lax.fori_loop(0, 2, forward_half, 0)
    pointwise(slope, False, through)
    store = pltpu.make_async_copy(through, through_hbm, store_sem.at[0])
    store.start()
    receive(2, 0)
    receive(2, 1)
    analyse_x(grads, SCALE_OUT)
    share(1, grads)
    back_mix()
    synthesise_x(3)
    weight_products()
    part_store = pltpu.make_async_copy(weight_part, weight_part_hbm, store_sem.at[1])
    part_store.start()
    store.wait()
    part_store.wait()
    for pair in range(2):
        wait_messages(3, pair)
        last[pair] = got[3, pair]
    for turn in range(4):
        for pair in range(2):
            pltpu.make_async_copy(
                sent.at[turn, pair, some], got.at[turn, pair, some], send_sem.at[turn, pair]
            ).wait()
    pltpu.make_async_copy(packed.at[three], packed.at[three], pack_sem.at[0]).wait()
    for kind in range(2):
        pltpu.make_async_copy(
            values.at[three], spectra.at[kind, three], part_sem.at[kind, 0]
        ).wait()


def last_kernel(
    messages, synthesis_z, synthesis_y, through_hbm, field_grad_hbm,
    grid, flat, result, through, field_grad, load_sem, store_sem,
):
    def some(pair, group):
        return (pl.ds(group * GROUP, GROUP), pl.ds(2 * pair, 2))

    def load(pair, group):
        return pltpu.make_async_copy(
            through_hbm.at[some(pair, group)], through.at[some(pair, group)],
            load_sem.at[pair, group],
        )

    def store(pair, group):
        return pltpu.make_async_copy(
            field_grad.at[some(pair, group)], field_grad_hbm.at[some(pair, group)],
            store_sem.at[pair, group],
        )

    for pair in range(2):
        for group in range(GROUPS):
            load(pair, group).start()

    def half(pair, carry):
        unpack(messages.at[pair], flat)
        synthesise_z(flat, grid, synthesis_z)

        def finish(group):
            load(pair, group).wait()

            def apply(offset, inner, part):
                place = (group * GROUP + offset, 2 * pair + inner)
                field_grad[place] = (through[place].astype(F32) + part * SCALE_IN).astype(BF16)

            each_plane(result, apply)
            store(pair, group).start()

        synthesise_y(grid, synthesis_y, result, finish)
        return carry

    lax.fori_loop(0, 2, half, 0)
    for pair in range(2):
        for group in range(GROUPS):
            store(pair, group).wait()


def body(fields, cotangent, local_weight, spectral_weight):
    shape = (C, WIDTH, NY, NZ)
    analysis_y, synthesis_y, analysis_z, synthesis_z, analysis_x, synthesis_x = make_tables()
    far = (
        fields.reshape(shape), cotangent.reshape(shape), spectral_weight,
        analysis_y, synthesis_y, synthesis_z,
    )
    near = (local_weight, analysis_z, analysis_x, synthesis_x)
    in_vmem, anywhere = pl.BlockSpec(memory_space=pltpu.VMEM), pl.BlockSpec(memory_space=pl.ANY)
    field_shape = jax.ShapeDtypeStruct(shape, BF16)
    message_shape = jax.ShapeDtypeStruct((2, SLABS, ROWS, LANES), BF16)
    part_shape = jax.ShapeDtypeStruct((C, C, LANES), F32)
    grid_shape = (MY, 2 * C, 2 * NZ)
    through, messages, part = pl.pallas_call(
        kernel,
        out_shape=(field_shape, message_shape, part_shape),
        in_specs=[anywhere] * len(far) + [in_vmem] * len(near),
        out_specs=[anywhere, in_vmem, anywhere],
        scratch_shapes=[pltpu.VMEM(array.shape, BF16) for array in far] + [
            pltpu.VMEM((4, 2, SLABS, ROWS, LANES), BF16),
            pltpu.VMEM((4, 2, SLABS, ROWS, LANES), BF16),
            pltpu.VMEM(grid_shape, F32),
            pltpu.VMEM((2, SLABS * ROWS, LANES), F32),
            pltpu.VMEM(shape, F32),
            pltpu.VMEM(shape, BF16),
            pltpu.VMEM(shape, BF16),
            pltpu.VMEM((BATCHES, C, C, LANES), BF16),
            pltpu.VMEM((BATCHES, 2, C, C, LANES), F32),
            pltpu.VMEM((BATCHES, C, LANES), F32),
            pltpu.VMEM((BATCHES, C, LANES), F32),
            pltpu.VMEM((BATCHES, C, LANES), F32),
            pltpu.VMEM((GROUP * NY, 2 * NZ), F32),
            pltpu.VMEM((C * BAND, C * BAND), BF16),
            pltpu.VMEM((2, BATCHES, C, LANES), F32),
            pltpu.VMEM((2, BATCHES, C, LANES), F32),
            pltpu.VMEM(part_shape.shape, F32),
            pltpu.SemaphoreType.DMA((4, 2)),
            pltpu.SemaphoreType.DMA((4, 2)),
            pltpu.SemaphoreType.DMA((4, 2)),
            pltpu.SemaphoreType.DMA((len(far) + 1,)),
            pltpu.SemaphoreType.DMA((2,)),
            pltpu.SemaphoreType.DMA((2,)),
            pltpu.SemaphoreType.DMA((2, 2)),
        ],
        compiler_params=pltpu.CompilerParams(
            collective_id=0, has_side_effects=True, vmem_limit_bytes=60 << 20
        ),
    )(*far, *near)
    field_grad = pl.pallas_call(
        last_kernel,
        out_shape=field_shape,
        in_specs=[in_vmem] * 3 + [anywhere],
        out_specs=anywhere,
        scratch_shapes=[
            pltpu.VMEM(grid_shape, F32),
            pltpu.VMEM((SLABS * ROWS, LANES), F32),
            pltpu.VMEM((GROUP * NY, 2 * NZ), F32),
            pltpu.VMEM(shape, BF16),
            pltpu.VMEM(shape, BF16),
            pltpu.SemaphoreType.DMA((2, GROUPS)),
            pltpu.SemaphoreType.DMA((2, GROUPS)),
        ],
        compiler_params=pltpu.CompilerParams(vmem_limit_bytes=60 << 20),
    )(messages, synthesis_z, synthesis_y, through)
    weight_grad = jnp.stack([part[:, :, :MODES], part[:, :, MODES:]], 0)
    return (field_grad.reshape(fields.shape), weight_grad)


def solution(mesh):
    placed = (
        P("batch", None, "slab", None, None),
        P("batch", None, "slab", None, None),
        P(),
        P(None, None, None, ("slab", "batch")),
    )
    return jax.shard_map(
        body,
        mesh=mesh,
        in_specs=placed,
        out_specs=(P("batch", None, "slab", None, None), P(None, None, None, ("slab", "batch"))),
        check_vma=False,
    )
```

time: 102 us -> 90 us (0.88)
  Pallas kernels: 99.5 us -> 87.9 us
    pallas_call x1, Pallas kernels: 89.9 us -> 79.3 us  [body(): pl.pallas_call(kernel, out_shape=(field_shape, message_shape, part_shape)...]
    pallas_call x1, Pallas kernels: 9.64 us -> 8.61 us  [body(): pl.pallas_call(last_kernel, out_shape=field_shape, in_specs=[in_vmem] * 3...]
where the time goes in v4:
time: 90 us; the launch traced here: 89.8 us
  Pallas kernels  87.9 us (98%)
  other arithmetic  1.08 us (1%)
    pallas_call x1, Pallas kernels, body(): pl.pallas_call(kernel, out_shape=(field_shape, message_shape, part_shape)...  79.3 us
    pallas_call x1, Pallas kernels, body(): pl.pallas_call(last_kernel, out_shape=field_shape, in_specs=[in_vmem] * 3...  8.61 us

profile of v4, /device:TPU:1, one launch (start us, length us, event | category | flops | bytes accessed | tf_op | source)
XLA Modules:
  0.0 89.8 jit_solution(6551573410292606422)
XLA Ops:
  0.6 79.3 %shard_map.113 = (bf16[32,4,128,128]{3,2,1,0:T(8,128)(2,1)}, bf16[2,64,8,128]{3,2,1,0:T(8,128)(2,1)}, f32[32,32,128]{2,1,0:T(8,128)}) custom-call(bf16[32,4,128,128]{3,2,1,0:T(8,128)(2,1)} %bitcast.7, bf16[32,4,128,128]{3,2,1,0:T(8,128)(2,1)} %bitcast.8, bf16[2,32,32,64]{3,2,1,0:T(8,128)(2,1)} %weights_hbm.1, ...), custom_call_target="tpu_custom_call" | custom-call | tf_op jit(solution)/shard_map/pallas_call | solution.py:598
  79.9 0.0 copy-start
  79.9 8.6 %shard_map.114 = bf16[32,4,128,128]{3,2,1,0:T(8,128)(2,1)} custom-call(bf16[2,64,8,128]{3,2,1,0:T(8,128)(2,1)} %get-tuple-element.5.messages, bf16[256,2048]{1,0:T(8,128)(2,1)} %constant.14.clone.synthesis_z_hbm.synthesis_z, bf16[1024,512]{1,0:T(8,128)(2,1)} %constant.13.clone.synthesis_y_hbm.synthesis_y, bf16[32,4,128,128]{3,2,1,0:T(8,128)(2,1)} %get-tuple-element.6.through_hbm), custom_call_target="tpu_custom_call" | custom-call | tf_op jit(solution)/shard_map/pallas_call | solution.py:633
  88.5 0.0 copy-done
  88.5 0.2 slice_bitcast_fusion.1
  88.7 1.1 %pad_maximum_fusion = f32[2,32,32,64]{3,2,1,0:T(8,128)} fusion(f32[1,32,32,64]{3,2,1,0:T(8,128)S(1)} %get-tuple-element.9, f32[1,32,32,64]{3,2,1,0:T(8,128)S(1)} %get-tuple-element.8), kind=kLoop, calls=%fused_computation | loop fusion | flops 131072 | bytes 1048576 | tf_op jit(solution)/shard_map/stack | solution.py:649
Async XLA Ops:
  79.9 8.6 %copy-start = (f32[32,32,128]{2,1,0:T(8,128)S(1)}, f32[32,32,128]{2,1,0:T(8,128)}, u32[]{:S(2)}) copy-start(f32[32,32,128]{2,1,0:T(8,128)} %get-tuple-element.7) | copy-start | bytes 1572868

commit v5 on v4

--- a/solution.py
+++ b/solution.py
@@ -28,6 +28,7 @@
 GROUPS = C // GROUP
 BAND = 16
 SOME_KY = 8
+AT_ONCE = 8
 MESH = pl.DeviceIdType.MESH
 F32 = jnp.float32
 BF16 = jnp.bfloat16
@@ -71,10 +72,9 @@
 
 
 def gelu_slope(values):
+    values = values.astype(BF16)
     size = jnp.abs(values)
-    below = 1.0 + (0.3275911 / math.sqrt(2.0)) * size
-    inverse = pl.reciprocal(below, approx=True)
-    inverse = inverse * (2.0 - below * inverse)
+    inverse = pl.reciprocal(1.0 + (0.3275911 / math.sqrt(2.0)) * size, approx=True)
     tail = 0.5 * 1.061405429 * inverse - 0.5 * 1.453152027
     tail = tail * inverse + 0.5 * 1.421413741
     tail = tail * inverse - 0.5 * 0.284496736
@@ -253,8 +253,9 @@
         left = lane_index((MZ, LANES)) < LANES // 2
 
         def transform(index):
-            batch = [(me // 2 + index * 4 + inner) % MY for inner in range(4)]
-            for two in (batch[:2], batch[2:]):
+            batch = [(me // 2 + index * AT_ONCE + inner) % MY for inner in range(AT_ONCE)]
+            for start in range(0, AT_ONCE, 2):
+                two = batch[start:start + 2]
                 first = jnp.concatenate([grid[ky] for ky in two], 0).astype(BF16)
                 second = lax.dot_general(
                     analysis_z[...], first, (((1,), (1,)), ((), ())), preferred_element_type=F32
@@ -271,18 +272,19 @@
                         ].astype(BF16)
             return batch
 
-        def step(index, carry):
-            for ky in transform(index):
+        def leave(batch):
+            for ky in batch:
                 for side in range(2):
                     send(turn, pair, 2 * ky + side)
-            return carry
-
-        for ky in transform(0)[1:]:
-            for side in range(2):
-                send(turn, pair, 2 * ky + side)
+
+        ready = transform(0)[1:]
+        for index in range(1, MY // AT_ONCE):
+            later = transform(index)
+            leave(ready)
+            ready = later
+        leave(ready)
         send(turn, pair, me + 1 - 2 * (me % 2))
         keep(turn, pair)
-        lax.fori_loop(1, MY // 4, step, 0)
 
     def analyse_x(target, scale):
         for block in range(BATCHES):
@@ -472,7 +474,7 @@
             def apply(offset, inner, part):
                 place = (group * GROUP + offset, 2 * pair + inner)
                 slopes = gelu_slope(linear[place] + part * SCALE_OUT)
-                slope[place] = (cotangent[place].astype(F32) * slopes).astype(BF16)
+                slope[place] = cotangent[place] * slopes
 
             each_plane(result, apply)
 

time: 90 us -> 85.2 us (0.947)
  Pallas kernels: 87.9 us -> 83 us
    pallas_call x1, Pallas kernels: 79.3 us -> 74.4 us  [body(): pl.pallas_call(kernel, out_shape=(field_shape, message_shape, part_shape)...]
where the time goes in v5:
time: 85.2 us; the launch traced here: 85 us
  Pallas kernels  83 us (97%)
  other arithmetic  1.08 us (1%)
    pallas_call x1, Pallas kernels, body(): pl.pallas_call(kernel, out_shape=(field_shape, message_shape, part_shape)...  74.4 us
    pallas_call x1, Pallas kernels, body(): pl.pallas_call(last_kernel, out_shape=field_shape, in_specs=[in_vmem] * 3...  8.61 us

profile of v5, /device:TPU:1, one launch (start us, length us, event | category | flops | bytes accessed | tf_op | source)
XLA Modules:
  0.0 85.0 jit_solution(17143517145891879396)
XLA Ops:
  0.6 74.4 %shard_map.113 = (bf16[32,4,128,128]{3,2,1,0:T(8,128)(2,1)}, bf16[2,64,8,128]{3,2,1,0:T(8,128)(2,1)}, f32[32,32,128]{2,1,0:T(8,128)}) custom-call(bf16[32,4,128,128]{3,2,1,0:T(8,128)(2,1)} %bitcast.7, bf16[32,4,128,128]{3,2,1,0:T(8,128)(2,1)} %bitcast.8, bf16[2,32,32,64]{3,2,1,0:T(8,128)(2,1)} %weights_hbm.1, ...), custom_call_target="tpu_custom_call" | custom-call | tf_op jit(solution)/shard_map/pallas_call | solution.py:600
  75.1 0.0 copy-start
  75.1 8.6 %shard_map.114 = bf16[32,4,128,128]{3,2,1,0:T(8,128)(2,1)} custom-call(bf16[2,64,8,128]{3,2,1,0:T(8,128)(2,1)} %get-tuple-element.5.messages, bf16[256,2048]{1,0:T(8,128)(2,1)} %constant.14.clone.synthesis_z_hbm.synthesis_z, bf16[1024,512]{1,0:T(8,128)(2,1)} %constant.13.clone.synthesis_y_hbm.synthesis_y, bf16[32,4,128,128]{3,2,1,0:T(8,128)(2,1)} %get-tuple-element.6.through_hbm), custom_call_target="tpu_custom_call" | custom-call | tf_op jit(solution)/shard_map/pallas_call | solution.py:635
  83.7 0.0 copy-done
  83.7 0.2 slice_bitcast_fusion.1
  83.9 1.1 %pad_maximum_fusion = f32[2,32,32,64]{3,2,1,0:T(8,128)} fusion(f32[1,32,32,64]{3,2,1,0:T(8,128)S(1)} %get-tuple-element.9, f32[1,32,32,64]{3,2,1,0:T(8,128)S(1)} %get-tuple-element.8), kind=kLoop, calls=%fused_computation | loop fusion | flops 131072 | bytes 1048576 | tf_op jit(solution)/shard_map/stack | solution.py:651
Async XLA Ops:
  75.1 8.6 %copy-start = (f32[32,32,128]{2,1,0:T(8,128)S(1)}, f32[32,32,128]{2,1,0:T(8,128)}, u32[]{:S(2)}) copy-start(f32[32,32,128]{2,1,0:T(8,128)} %get-tuple-element.7) | copy-start | bytes 1572868

commit v6 on v5

--- a/solution.py
+++ b/solution.py
@@ -505,9 +505,9 @@
     receive(0, 0)
     receive(0, 1)
     analyse_x(values, SCALE_IN)
-    share(0, values)
     mix()
     synthesise_x(1)
+    share(0, values)
     lax.fori_loop(0, 2, forward_half, 0)
     pointwise(slope, False, through)
     store = pltpu.make_async_copy(through, through_hbm, store_sem.at[0])
@@ -515,9 +515,9 @@
     receive(2, 0)
     receive(2, 1)
     analyse_x(grads, SCALE_OUT)
-    share(1, grads)
     back_mix()
     synthesise_x(3)
+    share(1, grads)
     weight_products()
     part_store = pltpu.make_async_copy(weight_part, weight_part_hbm, store_sem.at[1])
     part_store.start()

time: 85.2 us -> 85.1 us (level)
  no operation moved by 1% of the time
where the time goes in v6:
time: 85.1 us; the launch traced here: 84.9 us
  Pallas kernels  83 us (98%)
  other arithmetic  1.08 us (1%)
    pallas_call x1, Pallas kernels, body(): pl.pallas_call(kernel, out_shape=(field_shape, message_shape, part_shape)...  74.4 us
    pallas_call x1, Pallas kernels, body(): pl.pallas_call(last_kernel, out_shape=field_shape, in_specs=[in_vmem] * 3...  8.61 us

profile of v6, /device:TPU:1, one launch (start us, length us, event | category | flops | bytes accessed | tf_op | source)
XLA Modules:
  0.0 84.9 jit_solution(2659863402453583055)
XLA Ops:
  0.6 74.4 %shard_map.113 = (bf16[32,4,128,128]{3,2,1,0:T(8,128)(2,1)}, bf16[2,64,8,128]{3,2,1,0:T(8,128)(2,1)}, f32[32,32,128]{2,1,0:T(8,128)}) custom-call(bf16[32,4,128,128]{3,2,1,0:T(8,128)(2,1)} %bitcast.7, bf16[32,4,128,128]{3,2,1,0:T(8,128)(2,1)} %bitcast.8, bf16[2,32,32,64]{3,2,1,0:T(8,128)(2,1)} %weights_hbm.1, ...), custom_call_target="tpu_custom_call" | custom-call | tf_op jit(solution)/shard_map/pallas_call | solution.py:600
  75.0 0.0 copy-start
  75.0 8.6 %shard_map.114 = bf16[32,4,128,128]{3,2,1,0:T(8,128)(2,1)} custom-call(bf16[2,64,8,128]{3,2,1,0:T(8,128)(2,1)} %get-tuple-element.5.messages, bf16[256,2048]{1,0:T(8,128)(2,1)} %constant.14.clone.synthesis_z_hbm.synthesis_z, bf16[1024,512]{1,0:T(8,128)(2,1)} %constant.13.clone.synthesis_y_hbm.synthesis_y, bf16[32,4,128,128]{3,2,1,0:T(8,128)(2,1)} %get-tuple-element.6.through_hbm), custom_call_target="tpu_custom_call" | custom-call | tf_op jit(solution)/shard_map/pallas_call | solution.py:635
  83.6 0.0 copy-done
  83.6 0.2 slice_bitcast_fusion.1
  83.8 1.1 %pad_maximum_fusion = f32[2,32,32,64]{3,2,1,0:T(8,128)} fusion(f32[1,32,32,64]{3,2,1,0:T(8,128)S(1)} %get-tuple-element.9, f32[1,32,32,64]{3,2,1,0:T(8,128)S(1)} %get-tuple-element.8), kind=kLoop, calls=%fused_computation | loop fusion | flops 131072 | bytes 1048576 | tf_op jit(solution)/shard_map/stack | solution.py:651
Async XLA Ops:
  75.0 8.6 %copy-start = (f32[32,32,128]{2,1,0:T(8,128)S(1)}, f32[32,32,128]{2,1,0:T(8,128)}, u32[]{:S(2)}) copy-start(f32[32,32,128]{2,1,0:T(8,128)} %get-tuple-element.7) | copy-start | bytes 1572868
